TPU v7x, 512 devices: a whole 4x8x8 slice. The times are simulated.
512 devices in a mesh: ang: 32 (over z, x_lo, core), xy: 16 (over y, x_hi).
Axes of the slice: x: 4 (x_hi: 2, x_lo: 2; x = x_hi * 2 + x_lo), y: 8, z: 8, core: 2. Of those that a mesh axis runs over, the one named last changes fastest.
Arguments:
- contrast: float32 [32, 2, 1024, 2048], P('ang', None, 'xy'), may hold values from -4 to 4
- owners: int32 [3], replicated, may hold values from 0 to 31, as said below
- tilts: int32 [32, 2], P('ang'), may hold values from -8 to 8
Outputs:
- exit_real: float32 [32, 1024, 2048], P('ang', 'xy')
- exit_imag: float32 [32, 1024, 2048], P('ang', 'xy')
Inputs may be any that keep to these rules, and one draw needn't show every extreme that they name: `owners`: the 3 entries are distinct.
All inputs are finite; a program needn't handle non-finite values.
Results may differ from a plain program's by a relative error of at most 0.0003.
Values sent between devices are 32-bit elements; how exact they have to be, the bound alone decides.
No kernel may reach another device: no remote copies, remote signals or barrier semaphores. Data moves between devices by JAX's collectives and lax.ppermute only.
A program may use at most 64 MiB of HBM per device.

v0:
```python
import math

import jax
import jax.numpy as jnp
from jax import lax
from jax.sharding import PartitionSpec as P

diffraction = 0.05
phase_gain = 0.08


def from_root(value, axis, root):
    mine = lax.axis_index(axis) == root
    return lax.psum(jnp.where(mine, value, jnp.zeros_like(value)), axis)


def padded(cells, sides, width):
    for axis, dim in sides:
        count = lax.axis_size(axis)
        ends = count - 1
        head = lax.slice_in_dim(cells, 0, width, axis=dim)
        tail = lax.slice_in_dim(cells, cells.shape[dim] - width, cells.shape[dim], axis=dim)
        cells = jnp.concatenate(
            [
                lax.ppermute(tail, axis, [(i, (i + 1) % count) for i in range(ends)]),
                cells,
                lax.ppermute(head, axis, [((i + 1) % count, i) for i in range(ends)]),
            ],
            axis=dim,
        )
    return cells


def incident(tilts, first, rows, total_rows, cols):
    row_ids = first + jnp.arange(rows, dtype=jnp.int32)
    col_ids = jnp.arange(cols, dtype=jnp.int32)
    along_rows = tilts[:, 0:1] * row_ids[None, :] % total_rows
    along_cols = tilts[:, 1:2] * col_ids[None, :] % cols
    angle = 2.0 * math.pi * (along_rows.astype(jnp.float32) / total_rows)[:, :, None]
    angle = angle + 2.0 * math.pi * (along_cols.astype(jnp.float32) / cols)[:, None, :]
    return jnp.stack([jnp.cos(angle), jnp.sin(angle)])


def laplace(values):
    middle = values[..., 1:-1, :]
    widths = [(0, 0)] * (middle.ndim - 1) + [(1, 1)]
    sides = jnp.pad(middle, widths)
    return (
        values[..., :-2, :] + values[..., 2:, :] + sides[..., :-2] + sides[..., 2:] - 4.0 * middle
    )


def slope(values, plane):
    inner = diffraction * laplace(values) + phase_gain * plane * values[..., 1:-1, :]
    return jnp.stack([-inner[1], inner[0]])


def heun(field, plane_outer, plane_inner, valid_outer, valid_inner):
    first = slope(field, plane_outer)
    trial = (field[..., 1:-1, :] + first) * valid_outer
    second = slope(trial, plane_inner)
    return (field[..., 2:-2, :] + 0.5 * (first[..., 1:-1, :] + second)) * valid_inner


def inside(first, count, total_rows):
    row_ids = first + jnp.arange(count, dtype=jnp.int32)
    return ((row_ids >= 0) & (row_ids < total_rows)).astype(jnp.float32)[:, None]


def per_device(contrast, owners, tilts):
    depth = contrast.shape[1]
    rows = contrast.shape[2]
    cols = contrast.shape[3]
    total_rows = rows * lax.axis_size("xy")
    anchor = lax.axis_index("xy") * rows
    field = incident(tilts, anchor, rows, total_rows, cols)
    group = 1
    margin = 2 * group
    local = contrast[0]
    for slab_id in range(owners.shape[0]):
        root = owners[slab_id]
        slab = from_root(local, "ang", root)
        rimmed = padded(slab, (("xy", 1),), margin - 1)

        def fetch(j):
            return lax.dynamic_slice_in_dim(rimmed, j * group, group, 0)

        def advance(j, state):
            planes = fetch(j)
            current = padded(state, (("xy", 2),), margin)
            span = rows + 2 * margin - 2
            outer = planes[0, 0:span, :]
            start = anchor - margin
            valid_outer = inside(start + 1, span, total_rows)
            valid_inner = inside(start + 2, span - 2, total_rows)
            current = heun(current, outer, outer[1:-1], valid_outer, valid_inner)
            return current

        field = lax.fori_loop(0, depth // group, advance, field)
    return (field[0], field[1])


def solution(mesh):
    placed = (P("ang", None, "xy", None), P(), P("ang", None))
    return jax.shard_map(
        per_device,
        mesh=mesh,
        in_specs=placed,
        out_specs=(P("ang", "xy", None), P("ang", "xy", None)),
        check_vma=False,
    )
```

profile of v0, /device:TPU:48, one launch (start us, length us, event | category | flops | bytes accessed | tf_op | source)
XLA Modules:
  0.0 391.4 jit_solution(1693522457229782408)
XLA Ops:
  10.6 2.9 select_bitcast_fusion
  18.2 240.6 %all-reduce.9.cloned.1.call-done = (f32[2,64,2048]{2,1,0:T(8,128)}, f32[2,64,2048]{2,1,0:T(8,128)}, f32[2,64,2048]{2,1,0:T(8,128)}) async-done(((f32[2,64,2048]{2,1,0:T(8,128)}, f32[2,64,2048]{2,1,0:T(8,128)}, f32[2,64,2048]{2,1,0:T(8,128)}), (f32[2,64,2048]{2,1,0:T(8,128)}, f32[2,64,2048]{2,1,0:T(8,128)}, f32[2,64,2048]{2,1,0:T(8,128)})) %all-reduce.9.cloned.1.call-update) | async-done | bytes 3145744 | tf_op jit(solution)/shard_map/psum | solution.py:14
  259.8 5.5 %collective-permute-start.7 = (f32[2,1,2048]{2,1,0:T(1,128)S(1)}, f32[2,1,2048]{2,1,0:T(1,128)S(1)}, u32[]{:S(2)}, u32[]{:S(2)}) collective-permute-start(f32[2,1,2048]{2,1,0:T(1,128)S(1)} %get-tuple-element.420), channel_id=1, source_target_pairs={{1,0},{2,1},{3,2},{4,3},{5,4},{6,5},{7,6},{8,7},{9,8},{10,9},{11,1... | collective-permute-start | bytes 49160 | tf_op jit(solution)/shard_map/ppermute | solution.py:27
  268.3 6.5 %collective-permute-start.9 = (f32[2,1,2048]{2,1,0:T(1,128)S(1)}, f32[2,1,2048]{2,1,0:T(1,128)S(1)}, u32[]{:S(2)}, u32[]{:S(2)}) collective-permute-start(f32[2,1,2048]{2,1,0:T(1,128)S(1)} %get-tuple-element.418), channel_id=1, source_target_pairs={{1,0},{2,1},{3,2},{4,3},{5,4},{6,5},{7,6},{8,7},{9,8},{10,9},{11,1... | collective-permute-start | bytes 49160 | tf_op jit(solution)/shard_map/ppermute | solution.py:27
  277.7 6.3 %collective-permute-start.11 = (f32[2,1,2048]{2,1,0:T(1,128)S(1)}, f32[2,1,2048]{2,1,0:T(1,128)S(1)}, u32[]{:S(2)}, u32[]{:S(2)}) collective-permute-start(f32[2,1,2048]{2,1,0:T(1,128)S(1)} %get-tuple-element.416), channel_id=1, source_target_pairs={{1,0},{2,1},{3,2},{4,3},{5,4},{6,5},{7,6},{8,7},{9,8},{10,9},{11,1... | collective-permute-start | bytes 49160 | tf_op jit(solution)/shard_map/ppermute | solution.py:27
  289.5 2.5 collective-permute-done.10
  292.2 28.9 %while.45 = (s32[]{:T(128)}, f32[2,1,64,2048]{3,2,1,0:T(8,128)S(1)}, f32[2,66,2048]{2,1,0:T(8,128)}, s32[]{:T(128)}, s32[]{:T(128)}, /*index=5*/s32[]{:T(128)}, s32[]{:T(128)}, s32[]{}) while((s32[]{:T(128)}, f32[2,1,64,2048]{3,2,1,0:T(8,128)S(1)}, f32[2,66,2048]{2,1,0:T(8,128)}, s32[]{:T(128)}, s32[]{:T(128)}, /*index=5*/s32[]{:T(128)}, ...), condition=%wide.region_2.3_spmd, body=%wide.region_1.2_spmd.sunk | while | flops 8798861 | bytes 27116756 | solution.py:99
  292.2 4.2 %collective-permute-start = (f32[2,1,2,2048]{3,2,1,0:T(2,128)S(1)}, f32[2,1,2,2048]{3,2,1,0:T(2,128)S(1)}, u32[]{:S(2)}, u32[]{:S(2)}) collective-permute-start(f32[2,1,2,2048]{3,2,1,0:T(2,128)S(1)} %get-tuple-element.532), channel_id=1, source_target_pairs={{1,0},{2,1},{3,2},{4,3},{5,4},{6,5},{7,6},{8,7},{9,8},{10,9},{11,1... | collective-permute-start | bytes 98312 | tf_op jit(solution)/shard_map/while/body/eval_jaxpr/ppermute | solution.py:27
  296.4 3.2 collective-permute-start.1
  301.9 2.7 collective-permute-done.1
  307.2 3.1 collective-permute-start
  310.3 4.3 %collective-permute-start.1 = (f32[2,1,2,2048]{3,2,1,0:T(2,128)S(1)}, f32[2,1,2,2048]{3,2,1,0:T(2,128)S(1)}, u32[]{:S(2)}, u32[]{:S(2)}) collective-permute-start(f32[2,1,2,2048]{3,2,1,0:T(2,128)S(1)} %get-tuple-element.533), channel_id=1, source_target_pairs={{0,1},{1,2},{2,3},{3,4},{4,5},{5,6},{6,7},{7,8},{8,9},{9,10},{10,1... | collective-permute-start | bytes 98312 | tf_op jit(solution)/shard_map/while/body/eval_jaxpr/ppermute | solution.py:25
  321.1 31.8 %while.46 = (s32[]{:T(128)}, f32[2,1,64,2048]{3,2,1,0:T(8,128)S(1)}, f32[2,66,2048]{2,1,0:T(8,128)}, s32[]{:T(128)}, s32[]{:T(128)}, /*index=5*/s32[]{:T(128)}, s32[]{:T(128)}, s32[]{}) while((s32[]{:T(128)}, f32[2,1,64,2048]{3,2,1,0:T(8,128)S(1)}, f32[2,66,2048]{2,1,0:T(8,128)}, s32[]{:T(128)}, s32[]{:T(128)}, /*index=5*/s32[]{:T(128)}, ...), condition=%wide.region_5.6_spmd, body=%wide.region_4.5_spmd.sunk | while | flops 8798861 | bytes 27116756 | solution.py:99
  321.2 4.7 %collective-permute-start.2 = (f32[2,1,2,2048]{3,2,1,0:T(2,128)S(1)}, f32[2,1,2,2048]{3,2,1,0:T(2,128)S(1)}, u32[]{:S(2)}, u32[]{:S(2)}) collective-permute-start(f32[2,1,2,2048]{3,2,1,0:T(2,128)S(1)} %get-tuple-element.543), channel_id=1, source_target_pairs={{1,0},{2,1},{3,2},{4,3},{5,4},{6,5},{7,6},{8,7},{9,8},{10,9},{11,1... | collective-permute-start | bytes 98312 | tf_op jit(solution)/shard_map/while/body/eval_jaxpr/ppermute | solution.py:27
  325.9 2.6 collective-permute-start.3
  330.8 3.3 collective-permute-done.3
  336.7 5.4 %collective-permute-start.2 = (f32[2,1,2,2048]{3,2,1,0:T(2,128)S(1)}, f32[2,1,2,2048]{3,2,1,0:T(2,128)S(1)}, u32[]{:S(2)}, u32[]{:S(2)}) collective-permute-start(f32[2,1,2,2048]{3,2,1,0:T(2,128)S(1)} %get-tuple-element.543), channel_id=1, source_target_pairs={{1,0},{2,1},{3,2},{4,3},{5,4},{6,5},{7,6},{8,7},{9,8},{10,9},{11,1... | collective-permute-start | bytes 98312 | tf_op jit(solution)/shard_map/while/body/eval_jaxpr/ppermute | solution.py:27
  346.4 4.0 %collective-permute-done.3 = f32[2,1,2,2048]{3,2,1,0:T(2,128)S(1)} collective-permute-done((f32[2,1,2,2048]{3,2,1,0:T(2,128)S(1)}, f32[2,1,2,2048]{3,2,1,0:T(2,128)S(1)}, u32[]{:S(2)}, u32[]{:S(2)}) %collective-permute-start.3) | collective-permute-done | bytes 32800 | tf_op jit(solution)/shard_map/while/body/eval_jaxpr/ppermute | solution.py:25
  352.9 30.6 %while.47 = (s32[]{:T(128)}, f32[2,1,64,2048]{3,2,1,0:T(8,128)S(1)}, f32[2,66,2048]{2,1,0:T(8,128)S(1)}, s32[]{:T(128)}, s32[]{:T(128)}, /*index=5*/s32[]{:T(128)}, s32[]{:T(128)}, s32[]{}) while((s32[]{:T(128)}, f32[2,1,64,2048]{3,2,1,0:T(8,128)S(1)}, f32[2,66,2048]{2,1,0:T(8,128)S(1)}, s32[]{:T(128)}, s32[]{:T(128)}, /*index=5*/s32[]{:T(128)}, ...), condition=%wide.region_8.9_spmd, body=%wide.region_7.8_spmd.sunk | while | flops 8798861 | bytes 27116756 | solution.py:99
  353.0 5.4 %collective-permute-start.4 = (f32[2,1,2,2048]{3,2,1,0:T(2,128)S(1)}, f32[2,1,2,2048]{3,2,1,0:T(2,128)S(1)}, u32[]{:S(2)}, u32[]{:S(2)}) collective-permute-start(f32[2,1,2,2048]{3,2,1,0:T(2,128)S(1)} %get-tuple-element.554), channel_id=1, source_target_pairs={{1,0},{2,1},{3,2},{4,3},{5,4},{6,5},{7,6},{8,7},{9,8},{10,9},{11,1... | collective-permute-start | bytes 98312 | tf_op jit(solution)/shard_map/while/body/eval_jaxpr/ppermute | solution.py:27
  360.5 6.1 %collective-permute-done.5 = f32[2,1,2,2048]{3,2,1,0:T(2,128)S(1)} collective-permute-done((f32[2,1,2,2048]{3,2,1,0:T(2,128)S(1)}, f32[2,1,2,2048]{3,2,1,0:T(2,128)S(1)}, u32[]{:S(2)}, u32[]{:S(2)}) %collective-permute-start.5) | collective-permute-done | bytes 32800 | tf_op jit(solution)/shard_map/while/body/eval_jaxpr/ppermute | solution.py:25
  369.2 3.5 collective-permute-start.4
  372.8 3.8 collective-permute-start.5
  376.7 4.2 %collective-permute-done.5 = f32[2,1,2,2048]{3,2,1,0:T(2,128)S(1)} collective-permute-done((f32[2,1,2,2048]{3,2,1,0:T(2,128)S(1)}, f32[2,1,2,2048]{3,2,1,0:T(2,128)S(1)}, u32[]{:S(2)}, u32[]{:S(2)}) %collective-permute-start.5) | collective-permute-done | bytes 32800 | tf_op jit(solution)/shard_map/while/body/eval_jaxpr/ppermute | solution.py:25
  (116 shorter events, 49.6 us)
Async XLA Ops:
  7.2 251.6 %all-reduce.9.cloned.1.call-start = ((), (), s32[]{:S(2)}) async-start(), calls=%async_computation | async-start | bytes 6291456 | tf_op jit(solution)/shard_map/psum | solution.py:14
  13.6 0.7 copy-start.2
  259.8 24.2 %collective-permute-start.7 = (f32[2,1,2048]{2,1,0:T(1,128)S(1)}, f32[2,1,2048]{2,1,0:T(1,128)S(1)}, u32[]{:S(2)}, u32[]{:S(2)}) collective-permute-start(f32[2,1,2048]{2,1,0:T(1,128)S(1)} %get-tuple-element.420), channel_id=1, source_target_pairs={{1,0},{2,1},{3,2},{4,3},{5,4},{6,5},{7,6},{8,7},{9,8},{10,9},{11,1... | collective-permute-start | bytes 49160 | tf_op jit(solution)/shard_map/ppermute | solution.py:27
  265.3 20.6 %collective-permute-start.6 = (f32[2,1,2048]{2,1,0:T(1,128)S(1)}, f32[2,1,2048]{2,1,0:T(1,128)S(1)}, u32[]{:S(2)}, u32[]{:S(2)}) collective-permute-start(f32[2,1,2048]{2,1,0:T(1,128)S(1)} %get-tuple-element.419), channel_id=1, source_target_pairs={{0,1},{1,2},{2,3},{3,4},{4,5},{5,6},{6,7},{7,8},{8,9},{9,10},{10,1... | collective-permute-start | bytes 49160 | tf_op jit(solution)/shard_map/ppermute | solution.py:25
  268.3 20.1 %copy-start.1 = (f32[2,64,2048]{2,1,0:T(8,128)S(1)}, f32[2,64,2048]{2,1,0:T(8,128)}, u32[]{:S(2)}) copy-start(f32[2,64,2048]{2,1,0:T(8,128)} %get-tuple-element.393) | copy-start | bytes 3145732
  268.3 20.1 %collective-permute-start.9 = (f32[2,1,2048]{2,1,0:T(1,128)S(1)}, f32[2,1,2048]{2,1,0:T(1,128)S(1)}, u32[]{:S(2)}, u32[]{:S(2)}) collective-permute-start(f32[2,1,2048]{2,1,0:T(1,128)S(1)} %get-tuple-element.418), channel_id=1, source_target_pairs={{1,0},{2,1},{3,2},{4,3},{5,4},{6,5},{7,6},{8,7},{9,8},{10,9},{11,1... | collective-permute-start | bytes 49160 | tf_op jit(solution)/shard_map/ppermute | solution.py:27
  274.7 13.6 %collective-permute-start.8 = (f32[2,1,2048]{2,1,0:T(1,128)S(1)}, f32[2,1,2048]{2,1,0:T(1,128)S(1)}, u32[]{:S(2)}, u32[]{:S(2)}) collective-permute-start(f32[2,1,2048]{2,1,0:T(1,128)S(1)} %get-tuple-element.417), channel_id=1, source_target_pairs={{0,1},{1,2},{2,3},{3,4},{4,5},{5,6},{6,7},{7,8},{8,9},{9,10},{10,1... | collective-permute-start | bytes 49160 | tf_op jit(solution)/shard_map/ppermute | solution.py:25
  277.7 11.9 %collective-permute-start.11 = (f32[2,1,2048]{2,1,0:T(1,128)S(1)}, f32[2,1,2048]{2,1,0:T(1,128)S(1)}, u32[]{:S(2)}, u32[]{:S(2)}) collective-permute-start(f32[2,1,2048]{2,1,0:T(1,128)S(1)} %get-tuple-element.416), channel_id=1, source_target_pairs={{1,0},{2,1},{3,2},{4,3},{5,4},{6,5},{7,6},{8,7},{9,8},{10,9},{11,1... | collective-permute-start | bytes 49160 | tf_op jit(solution)/shard_map/ppermute | solution.py:27
  284.0 8.0 %collective-permute-start.10 = (f32[2,1,2048]{2,1,0:T(1,128)S(1)}, f32[2,1,2048]{2,1,0:T(1,128)S(1)}, u32[]{:S(2)}, u32[]{:S(2)}) collective-permute-start(f32[2,1,2048]{2,1,0:T(1,128)S(1)} %get-tuple-element.415), channel_id=1, source_target_pairs={{0,1},{1,2},{2,3},{3,4},{4,5},{5,6},{6,7},{7,8},{8,9},{9,10},{10,1... | collective-permute-start | bytes 49160 | tf_op jit(solution)/shard_map/ppermute | solution.py:25
  288.3 3.7 copy-start
  292.2 9.7 %collective-permute-start = (f32[2,1,2,2048]{3,2,1,0:T(2,128)S(1)}, f32[2,1,2,2048]{3,2,1,0:T(2,128)S(1)}, u32[]{:S(2)}, u32[]{:S(2)}) collective-permute-start(f32[2,1,2,2048]{3,2,1,0:T(2,128)S(1)} %get-tuple-element.532), channel_id=1, source_target_pairs={{1,0},{2,1},{3,2},{4,3},{5,4},{6,5},{7,6},{8,7},{9,8},{10,9},{11,1... | collective-permute-start | bytes 98312 | tf_op jit(solution)/shard_map/while/body/eval_jaxpr/ppermute | solution.py:27
  296.4 8.2 %collective-permute-start.1 = (f32[2,1,2,2048]{3,2,1,0:T(2,128)S(1)}, f32[2,1,2,2048]{3,2,1,0:T(2,128)S(1)}, u32[]{:S(2)}, u32[]{:S(2)}) collective-permute-start(f32[2,1,2,2048]{3,2,1,0:T(2,128)S(1)} %get-tuple-element.533), channel_id=1, source_target_pairs={{0,1},{1,2},{2,3},{3,4},{4,5},{5,6},{6,7},{7,8},{8,9},{9,10},{10,1... | collective-permute-start | bytes 98312 | tf_op jit(solution)/shard_map/while/body/eval_jaxpr/ppermute | solution.py:25
  307.2 9.7 %collective-permute-start = (f32[2,1,2,2048]{3,2,1,0:T(2,128)S(1)}, f32[2,1,2,2048]{3,2,1,0:T(2,128)S(1)}, u32[]{:S(2)}, u32[]{:S(2)}) collective-permute-start(f32[2,1,2,2048]{3,2,1,0:T(2,128)S(1)} %get-tuple-element.532), channel_id=1, source_target_pairs={{1,0},{2,1},{3,2},{4,3},{5,4},{6,5},{7,6},{8,7},{9,8},{10,9},{11,1... | collective-permute-start | bytes 98312 | tf_op jit(solution)/shard_map/while/body/eval_jaxpr/ppermute | solution.py:27
  310.3 8.2 %collective-permute-start.1 = (f32[2,1,2,2048]{3,2,1,0:T(2,128)S(1)}, f32[2,1,2,2048]{3,2,1,0:T(2,128)S(1)}, u32[]{:S(2)}, u32[]{:S(2)}) collective-permute-start(f32[2,1,2,2048]{3,2,1,0:T(2,128)S(1)} %get-tuple-element.533), channel_id=1, source_target_pairs={{0,1},{1,2},{2,3},{3,4},{4,5},{5,6},{6,7},{7,8},{8,9},{9,10},{10,1... | collective-permute-start | bytes 98312 | tf_op jit(solution)/shard_map/while/body/eval_jaxpr/ppermute | solution.py:25
  321.2 9.7 %collective-permute-start.2 = (f32[2,1,2,2048]{3,2,1,0:T(2,128)S(1)}, f32[2,1,2,2048]{3,2,1,0:T(2,128)S(1)}, u32[]{:S(2)}, u32[]{:S(2)}) collective-permute-start(f32[2,1,2,2048]{3,2,1,0:T(2,128)S(1)} %get-tuple-element.543), channel_id=1, source_target_pairs={{1,0},{2,1},{3,2},{4,3},{5,4},{6,5},{7,6},{8,7},{9,8},{10,9},{11,1... | collective-permute-start | bytes 98312 | tf_op jit(solution)/shard_map/while/body/eval_jaxpr/ppermute | solution.py:27
  325.9 8.2 %collective-permute-start.3 = (f32[2,1,2,2048]{3,2,1,0:T(2,128)S(1)}, f32[2,1,2,2048]{3,2,1,0:T(2,128)S(1)}, u32[]{:S(2)}, u32[]{:S(2)}) collective-permute-start(f32[2,1,2,2048]{3,2,1,0:T(2,128)S(1)} %get-tuple-element.544), channel_id=1, source_target_pairs={{0,1},{1,2},{2,3},{3,4},{4,5},{5,6},{6,7},{7,8},{8,9},{9,10},{10,1... | collective-permute-start | bytes 98312 | tf_op jit(solution)/shard_map/while/body/eval_jaxpr/ppermute | solution.py:25
  336.7 9.7 %collective-permute-start.2 = (f32[2,1,2,2048]{3,2,1,0:T(2,128)S(1)}, f32[2,1,2,2048]{3,2,1,0:T(2,128)S(1)}, u32[]{:S(2)}, u32[]{:S(2)}) collective-permute-start(f32[2,1,2,2048]{3,2,1,0:T(2,128)S(1)} %get-tuple-element.543), channel_id=1, source_target_pairs={{1,0},{2,1},{3,2},{4,3},{5,4},{6,5},{7,6},{8,7},{9,8},{10,9},{11,1... | collective-permute-start | bytes 98312 | tf_op jit(solution)/shard_map/while/body/eval_jaxpr/ppermute | solution.py:27
  342.1 8.2 %collective-permute-start.3 = (f32[2,1,2,2048]{3,2,1,0:T(2,128)S(1)}, f32[2,1,2,2048]{3,2,1,0:T(2,128)S(1)}, u32[]{:S(2)}, u32[]{:S(2)}) collective-permute-start(f32[2,1,2,2048]{3,2,1,0:T(2,128)S(1)} %get-tuple-element.544), channel_id=1, source_target_pairs={{0,1},{1,2},{2,3},{3,4},{4,5},{5,6},{6,7},{7,8},{8,9},{9,10},{10,1... | collective-permute-start | bytes 98312 | tf_op jit(solution)/shard_map/while/body/eval_jaxpr/ppermute | solution.py:25
  353.0 7.5 %collective-permute-start.4 = (f32[2,1,2,2048]{3,2,1,0:T(2,128)S(1)}, f32[2,1,2,2048]{3,2,1,0:T(2,128)S(1)}, u32[]{:S(2)}, u32[]{:S(2)}) collective-permute-start(f32[2,1,2,2048]{3,2,1,0:T(2,128)S(1)} %get-tuple-element.554), channel_id=1, source_target_pairs={{1,0},{2,1},{3,2},{4,3},{5,4},{6,5},{7,6},{8,7},{9,8},{10,9},{11,1... | collective-permute-start | bytes 98312 | tf_op jit(solution)/shard_map/while/body/eval_jaxpr/ppermute | solution.py:27
  358.4 8.2 %collective-permute-start.5 = (f32[2,1,2,2048]{3,2,1,0:T(2,128)S(1)}, f32[2,1,2,2048]{3,2,1,0:T(2,128)S(1)}, u32[]{:S(2)}, u32[]{:S(2)}) collective-permute-start(f32[2,1,2,2048]{3,2,1,0:T(2,128)S(1)} %get-tuple-element.555), channel_id=1, source_target_pairs={{0,1},{1,2},{2,3},{3,4},{4,5},{5,6},{6,7},{7,8},{8,9},{9,10},{10,1... | collective-permute-start | bytes 98312 | tf_op jit(solution)/shard_map/while/body/eval_jaxpr/ppermute | solution.py:25
  369.2 7.5 %collective-permute-start.4 = (f32[2,1,2,2048]{3,2,1,0:T(2,128)S(1)}, f32[2,1,2,2048]{3,2,1,0:T(2,128)S(1)}, u32[]{:S(2)}, u32[]{:S(2)}) collective-permute-start(f32[2,1,2,2048]{3,2,1,0:T(2,128)S(1)} %get-tuple-element.554), channel_id=1, source_target_pairs={{1,0},{2,1},{3,2},{4,3},{5,4},{6,5},{7,6},{8,7},{9,8},{10,9},{11,1... | collective-permute-start | bytes 98312 | tf_op jit(solution)/shard_map/while/body/eval_jaxpr/ppermute | solution.py:27
  372.8 8.2 %collective-permute-start.5 = (f32[2,1,2,2048]{3,2,1,0:T(2,128)S(1)}, f32[2,1,2,2048]{3,2,1,0:T(2,128)S(1)}, u32[]{:S(2)}, u32[]{:S(2)}) collective-permute-start(f32[2,1,2,2048]{3,2,1,0:T(2,128)S(1)} %get-tuple-element.555), channel_id=1, source_target_pairs={{0,1},{1,2},{2,3},{3,4},{4,5},{5,6},{6,7},{7,8},{8,9},{9,10},{10,1... | collective-permute-start | bytes 98312 | tf_op jit(solution)/shard_map/while/body/eval_jaxpr/ppermute | solution.py:25
Sparse Core Ops, SparseCore 0:
  13.7 245.0 all-reduce.8
where the time goes:
time: 393 us; the launch traced here: 391 us
  waiting for transfers between devices  265 us (67%)
  starting transfers between devices  68.2 us (17%)
  other arithmetic  33.8 us (9%)
  between operations  16.2 us (4%)
  local copies, waits for them, and re-layouts  7.44 us (2%)
    psum x1, waiting for transfers between devices, from_root(): return lax.psum(jnp.where(mine, value, jnp.zeros_like(value)), axis)  241 us
    ppermute x9, starting transfers between devices, padded(): lax.ppermute(head, axis, [((i + 1) % count, i) for i in range(ends)])  44.7 us
    ppermute x9, waiting for transfers between devices, padded(): lax.ppermute(tail, axis, [(i, (i + 1) % count) for i in range(ends)])  24.5 us
    ppermute x9, starting transfers between devices, padded(): lax.ppermute(tail, axis, [(i, (i + 1) % count) for i in range(ends)])  23.5 us
    mul x12, other arithmetic, slope(): phase_gain * plane * values[..., 1:-1, :]  9.27 us
    add x12, other arithmetic, slope(): diffraction * laplace(values) + phase_gain * plane * values[..., 1:-1, :]  8.05 us
  transfers between devices with their start and end apart: 19, of which 8 were waited for; matrix products, arithmetic and copies ran while one was open for 5% of the time, Pallas kernels for 0%

commit v1 on v0

v1 whole, which is shorter than its diff:
```python
import functools
import math

import jax
import jax.numpy as jnp
from jax import lax
from jax.experimental import pallas as pl
from jax.experimental.pallas import tpu as pltpu
from jax.sharding import PartitionSpec as P

diffraction = 0.05
phase_gain = 0.08

HALO = (12, 8, 4)
TOP = 24
ROWS = 112
LANES = 128

TRIAL = ((1, 13), (1, 13), (2, 12), (2, 12), (2, 12), (2, 12))
FIELD = ((1, 13), (2, 12), (2, 12), (2, 12), (2, 12), (3, 11))


def neighbours(tile, above, below, cols, row, lane):
    sums = []
    for c in range(cols):
        here = tile[c]
        zero = jnp.zeros_like(here)
        west = tile[c - 1] if c else zero
        east = tile[c + 1] if c < cols - 1 else zero
        up = pltpu.roll(jnp.where(row == 7, above[c], here), 1, 0)
        down = pltpu.roll(jnp.where(row == 0, below[c], here), 7, 0)
        left = pltpu.roll(jnp.where(lane == LANES - 1, west, here), 1, 1)
        right = pltpu.roll(jnp.where(lane == 0, east, here), LANES - 1, 1)
        sums.append((up + down) + (left + right))
    return sums


def load(ref, part, i, cols):
    at = pl.ds(pl.multiple_of(i * 8, 8), 8)
    return [ref[part, at, c * LANES : (c + 1) * LANES] for c in range(cols)]


def coupled(ref, part, i, plane, cols, row, lane):
    here = load(ref, part, i, cols)
    around = neighbours(here, load(ref, part, i - 1, cols), load(ref, part, i + 1, cols), cols, row, lane)
    return here, [s + p * h for s, p, h in zip(around, plane, here)]


def assemble(place, refs, planes, slab, skip, cols):
    count, to = 64 + 2 * HALO[slab], TOP - HALO[slab]
    for ref, core, half in refs:
        plane = place[1] if core == 0 else 1 - place[1]
        column = place[0] if half == 0 else 1 - place[0]
        for z in range(cols // 2):
            at = pl.ds(pl.multiple_of((2 * z + column) * LANES, LANES), LANES)
            values = ref[z, skip : skip + count, :]
            planes[plane, to : to + count, at] = (phase_gain / diffraction) * values - 4.0


def clear(refs):
    for ref in refs:
        blank = jnp.zeros((TOP,) + ref.shape[2:], jnp.float32)
        for part in range(2):
            ref[part, 0:TOP, :] = blank
            ref[part, TOP + 64 : ROWS, :] = blank


def advance(place, s, plane_ref, field, trial, after, cols):
    row = lax.broadcasted_iota(jnp.int32, (8, LANES), 0)
    lane = lax.broadcasted_iota(jnp.int32, (8, LANES), 1)
    low, high = bounds(place)

    def first(i, carry):
        at = pl.ds(pl.multiple_of(i * 8, 8), 8)
        plane = [plane_ref[at, c * LANES : (c + 1) * LANES] for c in range(cols)]
        re, a = coupled(field, 0, i, plane, cols, row, lane)
        for c in range(cols):
            span = slice(c * LANES, (c + 1) * LANES)
            trial[1, at, span] = field[1, at, span] + diffraction * a[c]
        im, b = coupled(field, 1, i, plane, cols, row, lane)
        for c in range(cols):
            span = slice(c * LANES, (c + 1) * LANES)
            trial[0, at, span] = re[c] - diffraction * b[c]
        return carry

    def second(i, carry):
        at = pl.ds(pl.multiple_of(i * 8, 8), 8)
        to = pl.ds(pl.multiple_of((i - after[1]) * 8, 8), 8)
        plane = [plane_ref[at, c * LANES : (c + 1) * LANES] for c in range(cols)]
        re, a = coupled(trial, 0, i, plane, cols, row, lane)
        for c in range(cols):
            span = slice(c * LANES, (c + 1) * LANES)
            old = field[1, at, span] + trial[1, at, span]
            after[0][1][to, span] = 0.5 * old + (0.5 * diffraction) * a[c]
        im, b = coupled(trial, 1, i, plane, cols, row, lane)
        for c in range(cols):
            span = slice(c * LANES, (c + 1) * LANES)
            old = field[0, at, span] + re[c]
            after[0][0][to, span] = 0.5 * old - (0.5 * diffraction) * b[c]
        return carry

    lax.fori_loop(jnp.maximum(low, TRIAL[s][0]), jnp.minimum(high, TRIAL[s][1]), first, 0)
    lax.fori_loop(jnp.maximum(low, FIELD[s][0]), jnp.minimum(high, FIELD[s][1]), second, 0)


def bounds(place):
    low = jnp.where(place[2] == 0, TOP // 8, 0)
    high = jnp.where(place[2] == place[3], TOP // 8 + 8, ROWS // 8)
    return low, high


def incident(rowwave, colwave, field, place, cols):
    low, high = bounds(place)

    def start(i, carry):
        at = pl.ds(pl.multiple_of(i * 8, 8), 8)
        c_row, s_row = rowwave[0, at, :], rowwave[1, at, :]
        for c in range(cols):
            span = slice(c * LANES, (c + 1) * LANES)
            c_col, s_col = colwave[0, :, span], colwave[1, :, span]
            field[0, at, span] = c_row * c_col - s_row * s_col
            field[1, at, span] = s_row * c_col + c_row * s_col
        return carry

    lax.fori_loop(jnp.maximum(low, 1), jnp.minimum(high, ROWS // 8 - 1), start, 0)


def through(*refs, slab, skip, cols, first, last):
    refs = list(refs)
    place = refs.pop(0)
    waves = [refs.pop(0) for _ in range(2)] if first else []
    before = None if first else refs.pop(0)
    mine, other, theirs = refs[:3]
    planes, trial, field = refs[-3:]
    pieces = ((mine, 0, 0), (other, 0, 1), (theirs.at[0], 1, 0), (theirs.at[1], 1, 1))
    assemble(place, pieces, planes, slab, skip, cols)
    clear((trial, field))
    if first:
        incident(*waves, field, place, cols)
        before = field
    middle = (field.at[0], field.at[1]), 0
    if last:
        after = (refs[3].at[0], refs[4].at[0]), TOP // 8
    else:
        clear((refs[3],))
        after = (refs[3].at[0], refs[3].at[1]), 0
    advance(place, 2 * slab, planes.at[0], before, trial, middle, cols)
    advance(place, 2 * slab + 1, planes.at[1], field, trial, after, cols)


def waves(tilts, anchor, total_rows, cols):
    row_ids = anchor - TOP + jnp.arange(ROWS, dtype=jnp.int32)
    col_ids = jnp.arange(cols, dtype=jnp.int32)
    along_rows = (tilts[0, 0] * row_ids) % total_rows
    along_cols = (tilts[0, 1] * col_ids) % cols
    row_angle = 2.0 * math.pi * (along_rows.astype(jnp.float32) / total_rows)
    col_angle = 2.0 * math.pi * (along_cols.astype(jnp.float32) / cols)
    by_row = jnp.stack([jnp.cos(row_angle), jnp.sin(row_angle)])
    by_col = jnp.stack([jnp.cos(col_angle), jnp.sin(col_angle)])
    return (
        jnp.broadcast_to(by_row[:, :, None], (2, ROWS, LANES)),
        jnp.broadcast_to(by_col[:, None, :], (2, 8, cols)),
    )


def keep(contrast, owners):
    rows, cols = contrast.shape[1:]
    angs = lax.axis_size("ang")
    chips = angs // 2
    chip = lax.axis_index("ang") // 2
    by_chip = [[2 * i + c for i in range(chips)] for c in range(2)]
    by_core = [[2 * i, 2 * i + 1] for i in range(chips)]
    planes = lax.all_to_all(contrast, "ang", 0, 0, tiled=True, axis_index_groups=by_core)
    owner_chip, owner_core = owners // 2, owners % 2

    def one():
        core = jnp.sum(jnp.where(owner_chip == chip, owner_core, 0))
        plane = lax.dynamic_index_in_dim(planes, core, 0, keepdims=False)
        tiles = plane.reshape(rows, chips, cols // chips).transpose(1, 0, 2)
        tiles = lax.all_to_all(tiles, "ang", 0, 0, tiled=True, axis_index_groups=by_chip)
        return tuple(lax.dynamic_index_in_dim(tiles, c, 0, keepdims=False) for c in owner_chip)

    def both():
        tiles = planes.reshape(2, rows, chips, cols // chips).transpose(2, 0, 1, 3)
        tiles = lax.all_to_all(tiles, "ang", 0, 0, tiled=True, axis_index_groups=by_chip)
        tiles = tiles.reshape(angs, rows, cols // chips)
        return tuple(lax.dynamic_index_in_dim(tiles, o, 0, keepdims=False) for o in owners)

    shared = (owner_chip[:, None] == owner_chip[None, :]).sum() > owners.shape[0]
    return lax.cond(shared, both, one)


def per_device(contrast, owners, tilts):
    depth, rows, cols = contrast.shape[1:]
    slabs = owners.shape[0]
    spots = lax.axis_size("xy")
    ang = lax.axis_index("ang")
    spot = lax.axis_index("xy")
    angs = lax.axis_size("ang")

    kept = keep(contrast[0], owners)

    tails = jnp.concatenate([kept[k][rows - HALO[k] :] for k in range(slabs)], axis=0)
    heads = jnp.concatenate([kept[k][: HALO[k]] for k in range(slabs)], axis=0)
    above = lax.ppermute(tails, "xy", [(i, i + 1) for i in range(spots - 1)])
    below = lax.ppermute(heads, "xy", [(i + 1, i) for i in range(spots - 1)])

    columns = [[4 * z + q for z in range(angs // 4)] for q in range(4)]
    swap_x = [(i, i ^ 2) for i in range(angs)]
    swap_core = [(i, i ^ 1) for i in range(angs)]

    def along_z(chosen, after=None):
        parts = []
        for k in chosen:
            at = slice(sum(HALO[:k]), sum(HALO[: k + 1]))
            parts += [above[at], kept[k], below[at]]
        piece = jnp.concatenate(parts, axis=0)
        if after is not None:
            piece, after = lax.optimization_barrier((piece, after))
        copies = jnp.broadcast_to(piece, (angs // 4,) + piece.shape)
        return lax.all_to_all(copies, "ang", 0, 0, tiled=True, axis_index_groups=columns)

    def from_core(mine, other):
        return lax.ppermute(jnp.stack([mine, other]), "ang", swap_core)

    early, late = (0, 1), (2,)
    mine = along_z(early)
    other = lax.ppermute(mine, "ang", swap_x)
    late_mine = along_z(late, mine)
    late_mine, other = lax.optimization_barrier((late_mine, other))
    late_other = lax.ppermute(late_mine, "ang", swap_x)
    first = mine, other, from_core(mine, other)

    by_row, by_col = waves(tilts, spot * rows, rows * spots, cols)
    place = jnp.stack([ang // 2 % 2, ang % 2, spot, jnp.int32(spots - 1)])

    def step(slab, before, pieces):
        start, end = slab == 0, slab == slabs - 1
        state = jax.ShapeDtypeStruct((2, ROWS, cols), jnp.float32)
        out = jax.ShapeDtypeStruct((1, rows, cols), jnp.float32)
        in_vmem = pl.BlockSpec(memory_space=pltpu.VMEM)
        return pl.pallas_call(
            functools.partial(
                through,
                slab=slab,
                skip=sum(rows + 2 * HALO[k] for k in early if k < slab) if slab in early else 0,
                cols=cols // LANES,
                first=start,
                last=end,
            ),
            out_shape=(out, out) if end else state,
            in_specs=[pl.BlockSpec(memory_space=pltpu.SMEM)] + [in_vmem] * (len(before) + len(pieces)),
            out_specs=(in_vmem, in_vmem) if end else in_vmem,
            scratch_shapes=[
                pltpu.VMEM((depth, ROWS, cols), jnp.float32),
                pltpu.VMEM(state.shape, jnp.float32),
                pltpu.VMEM(state.shape, jnp.float32),
            ],
            compiler_params=pltpu.CompilerParams(vmem_limit_bytes=32 * 1024 * 1024),
            cost_estimate=pl.CostEstimate(flops=20_000_000, bytes_accessed=6_000_000, transcendentals=0),
        )(place, *before, *pieces)

    field = step(0, (by_row, by_col), first)
    late_other, field = lax.optimization_barrier((late_other, field))
    last = late_mine, late_other, from_core(late_mine, late_other)
    field = step(1, (field,), first)
    return step(2, (field,), last)


def solution(mesh):
    placed = (P("ang", None, "xy", None), P(), P("ang", None))
    return jax.shard_map(
        per_device,
        mesh=mesh,
        in_specs=placed,
        out_specs=(P("ang", "xy", None), P("ang", "xy", None)),
        check_vma=False,
    )
```

time: 393 us -> 125 us (0.32)
  the two profiles are of different devices: /device:TPU:48 before, /device:TPU:33 now
where the time goes in v1:
time: 125 us; the launch traced here: 124 us
  starting transfers between devices  36.2 us (29%)
  blocking collectives  34.8 us (28%)
  Pallas kernels  21.2 us (17%)
  waiting for transfers between devices  15.6 us (12%)
  loops' own time  7.79 us (6%)
  other arithmetic  4.18 us (3%)
  local copies, waits for them, and re-layouts  2.85 us (2%)
  between operations  1.56 us (1%)
    all_to_all x2, blocking collectives, along_z(): lax.all_to_all(copies, 'ang', 0, 0, tiled=True, axis_index_groups=columns)  34.8 us
    pallas_call x3, Pallas kernels, step(): pl.pallas_call(functools.partial(through, slab=slab, skip=sum((rows + 2 *...  21.2 us
    all_to_all x1, starting transfers between devices, one(): lax.all_to_all(tiles, 'ang', 0, 0, tiled=True, axis_index_groups=by_chip)  11.1 us
    all_to_all x1, waiting for transfers between devices, one(): lax.all_to_all(tiles, 'ang', 0, 0, tiled=True, axis_index_groups=by_chip)  9.53 us
    ppermute x2, starting transfers between devices, from_core(): return lax.ppermute(jnp.stack([mine, other]), 'ang', swap_core)  9.13 us
    another operation x1, loops' own time, keep(): return lax.cond(shared, both, one)  7.79 us
    ppermute x1, waiting for transfers between devices, per_device(): above = lax.ppermute(tails, 'xy', [(i, i + 1) for i in range(spots - 1)])  5.47 us
    all_to_all x1, starting transfers between devices, keep(): lax.all_to_all(contrast, 'ang', 0, 0, tiled=True, axis_index_groups=by_core)  4.25 us
  transfers between devices with their start and end apart: 8, of which 4 were waited for; matrix products, arithmetic and copies ran while one was open for 3% of the time, Pallas kernels for 11%

profile of v1, /device:TPU:33, one launch (start us, length us, event | category | flops | bytes accessed | tf_op | source)
XLA Modules:
  0.0 124.1 jit_solution(4285507472418065181)
XLA Ops:
  0.6 4.3 %all-to-all-start.2 = ((f32[2,64,2048]{2,1,0:T(8,128)}), f32[2,64,2048]{2,1,0:T(8,128)S(1)}, u32[]{:S(2)}, u32[]{:S(2)}) async-start(f32[2,64,2048]{2,1,0:T(8,128)} %bitcast.75), calls=%async_computation.2 | async-start | bytes 2097152 | tf_op jit(solution)/shard_map/all_to_all | solution.py:173
  4.9 0.7 convert_reduce_fusion
  6.6 30.8 %conditional.1 = (f32[64,128]{1,0:T(8,128)S(1)}, f32[64,128]{1,0:T(8,128)S(1)}, f32[64,128]{1,0:T(8,128)S(1)}, f32[12,128]{1,0:T(8,128)S(1)}, f32[12,128]{1,0:T(...) conditional(s32[]{:T(128)} %convert_element_type.35, ...), branch_computations={%region_1.3_spmd, %region_3.4_spmd} | conditional | flops 38 | bytes 5488942 | solution.py:190
  6.6 0.6 fusion.2
  9.4 1.0 copy.9
  10.3 11.1 %all-to-all-start = ((f32[16,64,128]{2,1,0:T(8,128)}), f32[16,64,128]{2,1,0:T(8,128)S(1)}, u32[]{:S(2)}, u32[]{:S(2)}) async-start(f32[16,64,128]{2,1,0:T(8,128)} %copy.9), calls=%async_computation | async-start | bytes 1048576 | tf_op jit(solution)/shard_map/cond/branch_0_fun/all_to_all | solution.py:180
  21.4 0.7 fusion.15
  27.9 9.5 %all-to-all-done = f32[16,64,128]{2,1,0:T(8,128)S(1)} async-done(((f32[16,64,128]{2,1,0:T(8,128)}), f32[16,64,128]{2,1,0:T(8,128)S(1)}, u32[]{:S(2)}, u32[]{:S(2)}) %all-to-all-start) | async-done | bytes 524320 | tf_op jit(solution)/shard_map/cond/branch_0_fun/all_to_all | solution.py:180
  37.5 4.2 %collective-permute-start.1 = (f32[24,128]{1,0:T(8,128)S(1)}, f32[24,128]{1,0:T(8,128)S(1)}, u32[]{:S(2)}, u32[]{:S(2)}) collective-permute-start(f32[24,128]{1,0:T(8,128)S(1)} %pad_maximum_fusion.5), channel_id=1, source_target_pairs={{1,0},{2,1},{3,2},{4,3},{5,4},{6,5},{7,6},{8,7},{9,8},{10,9},{11,1... | collective-permute-start | bytes 36872 | tf_op jit(solution)/shard_map/ppermute | solution.py:206
  41.8 2.5 %collective-permute-start = (f32[24,128]{1,0:T(8,128)S(1)}, f32[24,128]{1,0:T(8,128)S(1)}, u32[]{:S(2)}, u32[]{:S(2)}) collective-permute-start(f32[24,128]{1,0:T(8,128)S(1)} %pad_maximum_fusion.4), channel_id=1, source_target_pairs={{0,1},{1,2},{2,3},{3,4},{4,5},{5,6},{6,7},{7,8},{8,9},{9,10},{10,1... | collective-permute-start | bytes 36872 | tf_op jit(solution)/shard_map/ppermute | solution.py:205
  44.3 5.5 %collective-permute-done = f32[24,128]{1,0:T(8,128)S(1)} collective-permute-done((f32[24,128]{1,0:T(8,128)S(1)}, f32[24,128]{1,0:T(8,128)S(1)}, u32[]{:S(2)}, u32[]{:S(2)}) %collective-permute-start) | collective-permute-done | bytes 12320 | tf_op jit(solution)/shard_map/ppermute | solution.py:205
  50.1 22.1 %all_to_all.23.refs_3_.refs_2_ = f32[8,168,128]{2,1,0:T(8,128)S(1)} all-to-all(f32[8,168,128]{2,1,0:T(8,128)S(1)} %broadcast_in_dim.12), channel_id=1, replica_groups={{0,64,128,192,256,320,384,448},{16,80,144,208,272,336,400,464},{32,96,1..., dimensions={0} | all-to-all | bytes 1376256 | tf_op jit(solution)/shard_map/all_to_all | solution.py:221
  72.3 1.9 %collective-permute-start.2 = (f32[8,168,128]{2,1,0:T(8,128)S(1)}, f32[8,168,128]{2,1,0:T(8,128)S(1)}, u32[]{:S(2)}, u32[]{:S(2)}) collective-permute-start(f32[8,168,128]{2,1,0:T(8,128)S(1)} %all_to_all.23.refs_3_.refs_2_), channel_id=1, source_target_pairs={{0,32},{16,48},{32,0},{48,16},{64,96},{80,112},{96,64},{112,80},{1... | collective-permute-start | bytes 2064392 | tf_op jit(solution)/shard_map/ppermute | solution.py:228
  74.2 12.7 %all_to_all.24.refs_2_ = f32[8,72,128]{2,1,0:T(8,128)S(1)} all-to-all(f32[8,72,128]{2,1,0:T(8,128)S(1)} %broadcast_in_dim.13), channel_id=1, replica_groups={{0,64,128,192,256,320,384,448},{16,80,144,208,272,336,400,464},{32,96,1..., dimensions={0} | all-to-all | bytes 589824 | tf_op jit(solution)/shard_map/all_to_all | solution.py:221
  87.1 1.2 pad_maximum_fusion
  88.3 6.8 %collective-permute-start.4 = (f32[2,8,168,128]{3,2,1,0:T(8,128)}, f32[2,8,168,128]{3,2,1,0:T(8,128)S(1)}, u32[]{:S(2)}, u32[]{:S(2)}) collective-permute-start(f32[2,8,168,128]{3,2,1,0:T(8,128)} %pad_maximum_fusion), channel_id=1, source_target_pairs={{0,16},{16,0},{32,48},{48,32},{64,80},{80,64},{96,112},{112,96},{1... | collective-permute-start | bytes 4128776 | tf_op jit(solution)/shard_map/ppermute | solution.py:224
  95.1 0.6 fusion.17
  95.7 0.6 fusion.13
  96.4 0.8 fusion.8
  97.2 3.1 %collective-permute-start.3 = (f32[8,72,128]{2,1,0:T(8,128)S(1)}, f32[8,72,128]{2,1,0:T(8,128)S(1)}, u32[]{:S(2)}, u32[]{:S(2)}) collective-permute-start(f32[8,72,128]{2,1,0:T(8,128)S(1)} %all_to_all.24.refs_2_), channel_id=1, source_target_pairs={{0,32},{16,48},{32,0},{48,16},{64,96},{80,112},{96,64},{112,80},{1... | collective-permute-start | bytes 884744 | tf_op jit(solution)/shard_map/ppermute | solution.py:231
  100.5 7.6 %shard_map.50.refs_1_ = f32[2,112,2048]{2,1,0:T(8,128)S(1)} custom-call(s32[4]{0:T(128)S(1)} %pad_add_fusion.refs_0_, f32[2,112,128]{2,1,0:T(8,128)S(1)} %broadcast_in_dim.26.refs_1_, f32[2,8,2048]{2,1,0:T(8,128)S(1)} %broadcast_in_dim.27.refs_2_, f32[8,168,128]{2,1,0:T(8,128)S(1)} %all_to_all.23.refs_3_.refs_2_, ...), custom_call_target="tpu_custom_call" | custom-call | flops 20000000 | bytes 6000000 | tf_op jit(solution)/shard_map/pallas_call | solution.py:242
  108.1 2.4 %collective-permute-start.5 = (f32[2,8,72,128]{3,2,1,0:T(8,128)S(1)}, f32[2,8,72,128]{3,2,1,0:T(8,128)S(1)}, u32[]{:S(2)}, u32[]{:S(2)}) collective-permute-start(f32[2,8,72,128]{3,2,1,0:T(8,128)S(1)} %pad_maximum_fusion.1), channel_id=1, source_target_pairs={{0,16},{16,0},{32,48},{48,32},{64,80},{80,64},{96,112},{112,96},{1... | collective-permute-start | bytes 1769480 | tf_op jit(solution)/shard_map/ppermute | solution.py:224
  110.5 6.5 %shard_map.51.refs_1_ = f32[2,112,2048]{2,1,0:T(8,128)S(1)} custom-call(s32[4]{0:T(128)S(1)} %pad_add_fusion.refs_0_, f32[2,112,2048]{2,1,0:T(8,128)S(1)} %shard_map.50.refs_1_, f32[8,168,128]{2,1,0:T(8,128)S(1)} %all_to_all.23.refs_3_.refs_2_, f32[8,168,128]{2,1,0:T(8,128)S(1)} %collective-permute-done.2.refs_4_.refs_3_, ...), custom_call_target="tpu_custom_call" | custom-call | flops 20000000 | bytes 6000000 | tf_op jit(solution)/shard_map/pallas_call | solution.py:242
  117.0 7.1 %shard_map.52 = (f32[1,64,2048]{2,1,0:T(8,128)}, f32[1,64,2048]{2,1,0:T(8,128)}) custom-call(s32[4]{0:T(128)S(1)} %pad_add_fusion.refs_0_, f32[2,112,2048]{2,1,0:T(8,128)S(1)} %shard_map.51.refs_1_, f32[8,72,128]{2,1,0:T(8,128)S(1)} %all_to_all.24.refs_2_, f32[8,72,128]{2,1,0:T(8,128)S(1)} %collective-permute-done.3.refs_3_, ...), custom_call_target="tpu_custom_call" | custom-call | flops 20000000 | bytes 6000000 | tf_op jit(solution)/shard_map/pallas_call | solution.py:242
  (35 shorter events, 1.4 us)
Async XLA Ops:
  0.6 4.3 %copy-start = (s32[3]{0:T(128)S(1)}, s32[3]{0:T(128)}, u32[]{:S(2)}) copy-start(s32[3]{0:T(128)} %param.6) | copy-start | bytes 40
  0.6 6.0 %all-to-all-start.2 = ((f32[2,64,2048]{2,1,0:T(8,128)}), f32[2,64,2048]{2,1,0:T(8,128)S(1)}, u32[]{:S(2)}, u32[]{:S(2)}) async-start(f32[2,64,2048]{2,1,0:T(8,128)} %bitcast.75), calls=%async_computation.2 | async-start | bytes 2097152 | tf_op jit(solution)/shard_map/all_to_all | solution.py:173
  10.3 27.1 %all-to-all-start = ((f32[16,64,128]{2,1,0:T(8,128)}), f32[16,64,128]{2,1,0:T(8,128)S(1)}, u32[]{:S(2)}, u32[]{:S(2)}) async-start(f32[16,64,128]{2,1,0:T(8,128)} %copy.9), calls=%async_computation | async-start | bytes 1048576 | tf_op jit(solution)/shard_map/cond/branch_0_fun/all_to_all | solution.py:180
  37.5 6.8 %collective-permute-start.1 = (f32[24,128]{1,0:T(8,128)S(1)}, f32[24,128]{1,0:T(8,128)S(1)}, u32[]{:S(2)}, u32[]{:S(2)}) collective-permute-start(f32[24,128]{1,0:T(8,128)S(1)} %pad_maximum_fusion.5), channel_id=1, source_target_pairs={{1,0},{2,1},{3,2},{4,3},{5,4},{6,5},{7,6},{8,7},{9,8},{10,9},{11,1... | collective-permute-start | bytes 36872 | tf_op jit(solution)/shard_map/ppermute | solution.py:206
  41.8 8.1 %collective-permute-start = (f32[24,128]{1,0:T(8,128)S(1)}, f32[24,128]{1,0:T(8,128)S(1)}, u32[]{:S(2)}, u32[]{:S(2)}) collective-permute-start(f32[24,128]{1,0:T(8,128)S(1)} %pad_maximum_fusion.4), channel_id=1, source_target_pairs={{0,1},{1,2},{2,3},{3,4},{4,5},{5,6},{6,7},{7,8},{8,9},{9,10},{10,1... | collective-permute-start | bytes 36872 | tf_op jit(solution)/shard_map/ppermute | solution.py:205
  72.3 14.8 %collective-permute-start.2 = (f32[8,168,128]{2,1,0:T(8,128)S(1)}, f32[8,168,128]{2,1,0:T(8,128)S(1)}, u32[]{:S(2)}, u32[]{:S(2)}) collective-permute-start(f32[8,168,128]{2,1,0:T(8,128)S(1)} %all_to_all.23.refs_3_.refs_2_), channel_id=1, source_target_pairs={{0,32},{16,48},{32,0},{48,16},{64,96},{80,112},{96,64},{112,80},{1... | collective-permute-start | bytes 2064392 | tf_op jit(solution)/shard_map/ppermute | solution.py:228
  87.1 8.0 %copy-start.1 = (s32[1,2]{1,0:T(1,128)S(1)}, s32[1,2]{1,0:T(1,128)}, u32[]{:S(2)}) copy-start(s32[1,2]{1,0:T(1,128)} %param.7) | copy-start | bytes 28
  88.3 12.1 %collective-permute-start.4 = (f32[2,8,168,128]{3,2,1,0:T(8,128)}, f32[2,8,168,128]{3,2,1,0:T(8,128)S(1)}, u32[]{:S(2)}, u32[]{:S(2)}) collective-permute-start(f32[2,8,168,128]{3,2,1,0:T(8,128)} %pad_maximum_fusion), channel_id=1, source_target_pairs={{0,16},{16,0},{32,48},{48,32},{64,80},{80,64},{96,112},{112,96},{1... | collective-permute-start | bytes 4128776 | tf_op jit(solution)/shard_map/ppermute | solution.py:224
  97.2 10.9 %collective-permute-start.3 = (f32[8,72,128]{2,1,0:T(8,128)S(1)}, f32[8,72,128]{2,1,0:T(8,128)S(1)}, u32[]{:S(2)}, u32[]{:S(2)}) collective-permute-start(f32[8,72,128]{2,1,0:T(8,128)S(1)} %all_to_all.24.refs_2_), channel_id=1, source_target_pairs={{0,32},{16,48},{32,0},{48,16},{64,96},{80,112},{96,64},{112,80},{1... | collective-permute-start | bytes 884744 | tf_op jit(solution)/shard_map/ppermute | solution.py:231
  108.1 8.9 %collective-permute-start.5 = (f32[2,8,72,128]{3,2,1,0:T(8,128)S(1)}, f32[2,8,72,128]{3,2,1,0:T(8,128)S(1)}, u32[]{:S(2)}, u32[]{:S(2)}) collective-permute-start(f32[2,8,72,128]{3,2,1,0:T(8,128)S(1)} %pad_maximum_fusion.1), channel_id=1, source_target_pairs={{0,16},{16,0},{32,48},{48,32},{64,80},{80,64},{96,112},{112,96},{1... | collective-permute-start | bytes 1769480 | tf_op jit(solution)/shard_map/ppermute | solution.py:224

commit v2 on v1

--- a/solution.py
+++ b/solution.py
@@ -57,18 +57,21 @@
             planes[plane, to : to + count, at] = (phase_gain / diffraction) * values - 4.0
 
 
-def clear(refs):
-    for ref in refs:
-        blank = jnp.zeros((TOP,) + ref.shape[2:], jnp.float32)
-        for part in range(2):
-            ref[part, 0:TOP, :] = blank
-            ref[part, TOP + 64 : ROWS, :] = blank
+def clear_outside(place, parts):
+    @pl.when(place[2] == 0)
+    def _():
+        for ref in parts:
+            ref[0:TOP, :] = jnp.zeros((TOP, ref.shape[1]), jnp.float32)
+
+    @pl.when(place[2] == place[3])
+    def _():
+        for ref in parts:
+            ref[TOP + 64 : ROWS, :] = jnp.zeros((ROWS - TOP - 64, ref.shape[1]), jnp.float32)
 
 
 def advance(place, s, plane_ref, field, trial, after, cols):
     row = lax.broadcasted_iota(jnp.int32, (8, LANES), 0)
     lane = lax.broadcasted_iota(jnp.int32, (8, LANES), 1)
-    low, high = bounds(place)
 
     def first(i, carry):
         at = pl.ds(pl.multiple_of(i * 8, 8), 8)
@@ -99,19 +102,12 @@
             after[0][0][to, span] = 0.5 * old - (0.5 * diffraction) * b[c]
         return carry
 
-    lax.fori_loop(jnp.maximum(low, TRIAL[s][0]), jnp.minimum(high, TRIAL[s][1]), first, 0)
-    lax.fori_loop(jnp.maximum(low, FIELD[s][0]), jnp.minimum(high, FIELD[s][1]), second, 0)
-
-
-def bounds(place):
-    low = jnp.where(place[2] == 0, TOP // 8, 0)
-    high = jnp.where(place[2] == place[3], TOP // 8 + 8, ROWS // 8)
-    return low, high
-
-
-def incident(rowwave, colwave, field, place, cols):
-    low, high = bounds(place)
-
+    lax.fori_loop(*TRIAL[s], first, 0, unroll=True)
+    clear_outside(place, (trial.at[0], trial.at[1]))
+    lax.fori_loop(*FIELD[s], second, 0, unroll=True)
+
+
+def incident(rowwave, colwave, field, cols):
     def start(i, carry):
         at = pl.ds(pl.multiple_of(i * 8, 8), 8)
         c_row, s_row = rowwave[0, at, :], rowwave[1, at, :]
@@ -122,7 +118,7 @@
             field[1, at, span] = s_row * c_col + c_row * s_col
         return carry
 
-    lax.fori_loop(jnp.maximum(low, 1), jnp.minimum(high, ROWS // 8 - 1), start, 0)
+    lax.fori_loop(0, ROWS // 8, start, 0, unroll=2)
 
 
 def through(*refs, slab, skip, cols, first, last):
@@ -134,18 +130,18 @@
     planes, trial, field = refs[-3:]
     pieces = ((mine, 0, 0), (other, 0, 1), (theirs.at[0], 1, 0), (theirs.at[1], 1, 1))
     assemble(place, pieces, planes, slab, skip, cols)
-    clear((trial, field))
     if first:
-        incident(*waves, field, place, cols)
+        incident(*waves, field, cols)
         before = field
-    middle = (field.at[0], field.at[1]), 0
+    middle = field.at[0], field.at[1]
+    advance(place, 2 * slab, planes.at[0], before, trial, (middle, 0), cols)
+    clear_outside(place, middle)
     if last:
-        after = (refs[3].at[0], refs[4].at[0]), TOP // 8
+        advance(place, 2 * slab + 1, planes.at[1], field, trial, ((refs[3].at[0], refs[4].at[0]), TOP // 8), cols)
     else:
-        clear((refs[3],))
-        after = (refs[3].at[0], refs[3].at[1]), 0
-    advance(place, 2 * slab, planes.at[0], before, trial, middle, cols)
-    advance(place, 2 * slab + 1, planes.at[1], field, trial, after, cols)
+        after = refs[3].at[0], refs[3].at[1]
+        advance(place, 2 * slab + 1, planes.at[1], field, trial, (after, 0), cols)
+        clear_outside(place, after)
 
 
 def waves(tilts, anchor, total_rows, cols):
@@ -155,7 +151,8 @@
     along_cols = (tilts[0, 1] * col_ids) % cols
     row_angle = 2.0 * math.pi * (along_rows.astype(jnp.float32) / total_rows)
     col_angle = 2.0 * math.pi * (along_cols.astype(jnp.float32) / cols)
-    by_row = jnp.stack([jnp.cos(row_angle), jnp.sin(row_angle)])
+    inside = (row_ids >= 0) & (row_ids < total_rows)
+    by_row = jnp.where(inside, jnp.stack([jnp.cos(row_angle), jnp.sin(row_angle)]), 0.0)
     by_col = jnp.stack([jnp.cos(col_angle), jnp.sin(col_angle)])
     return (
         jnp.broadcast_to(by_row[:, :, None], (2, ROWS, LANES)),
@@ -227,11 +224,11 @@
     mine = along_z(early)
     other = lax.ppermute(mine, "ang", swap_x)
     late_mine = along_z(late, mine)
-    late_mine, other = lax.optimization_barrier((late_mine, other))
+    late_mine, other, tilts = lax.optimization_barrier((late_mine, other, tilts))
     late_other = lax.ppermute(late_mine, "ang", swap_x)
     first = mine, other, from_core(mine, other)
 
-    by_row, by_col = waves(tilts, spot * rows, rows * spots, cols)
+    wave = waves(tilts, spot * rows, rows * spots, cols)
     place = jnp.stack([ang // 2 % 2, ang % 2, spot, jnp.int32(spots - 1)])
 
     def step(slab, before, pieces):
@@ -260,11 +257,9 @@
             cost_estimate=pl.CostEstimate(flops=20_000_000, bytes_accessed=6_000_000, transcendentals=0),
         )(place, *before, *pieces)
 
-    field = step(0, (by_row, by_col), first)
+    field = step(1, (step(0, wave, first),), first)
     late_other, field = lax.optimization_barrier((late_other, field))
-    last = late_mine, late_other, from_core(late_mine, late_other)
-    field = step(1, (field,), first)
-    return step(2, (field,), last)
+    return step(2, (field,), (late_mine, late_other, from_core(late_mine, late_other)))
 
 
 def solution(mesh):

time: 125 us -> 118 us (0.944)
  the two profiles are of different devices: /device:TPU:33 before, /device:TPU:29 now
where the time goes in v2:
time: 118 us; the launch traced here: 117 us
  starting transfers between devices  36.3 us (31%)
  blocking collectives  34.4 us (29%)
  waiting for transfers between devices  17.5 us (15%)
  Pallas kernels  12.6 us (11%)
  loops' own time  7.8 us (7%)
  other arithmetic  4.37 us (4%)
  local copies, waits for them, and re-layouts  2.85 us (2%)
  between operations  1.56 us (1%)
    all_to_all x2, blocking collectives, along_z(): lax.all_to_all(copies, 'ang', 0, 0, tiled=True, axis_index_groups=columns)  34.4 us
    pallas_call x3, Pallas kernels, step(): pl.pallas_call(functools.partial(through, slab=slab, skip=sum((rows + 2 *...  12.6 us
    all_to_all x1, starting transfers between devices, one(): lax.all_to_all(tiles, 'ang', 0, 0, tiled=True, axis_index_groups=by_chip)  10.8 us
    all_to_all x1, waiting for transfers between devices, one(): lax.all_to_all(tiles, 'ang', 0, 0, tiled=True, axis_index_groups=by_chip)  9.53 us
    ppermute x2, starting transfers between devices, from_core(): return lax.ppermute(jnp.stack([mine, other]), 'ang', swap_core)  9.27 us
    another operation x1, loops' own time, keep(): return lax.cond(shared, both, one)  7.8 us
    ppermute x1, waiting for transfers between devices, per_device(): below = lax.ppermute(heads, 'xy', [(i + 1, i) for i in range(spots - 1)])  5.88 us
    ppermute x1, starting transfers between devices, per_device(): above = lax.ppermute(tails, 'xy', [(i, i + 1) for i in range(spots - 1)])  4.65 us
  transfers between devices with their start and end apart: 8, of which 4 were waited for; matrix products, arithmetic and copies ran while one was open for 3% of the time, Pallas kernels for 7%

profile of v2, /device:TPU:29, one launch (start us, length us, event | category | flops | bytes accessed | tf_op | source)
XLA Modules:
  0.0 117.4 jit_solution(12811565552578852197)
XLA Ops:
  0.6 4.3 %all-to-all-start.2 = ((f32[2,64,2048]{2,1,0:T(8,128)}), f32[2,64,2048]{2,1,0:T(8,128)S(1)}, u32[]{:S(2)}, u32[]{:S(2)}) async-start(f32[2,64,2048]{2,1,0:T(8,128)} %bitcast.75), calls=%async_computation.2 | async-start | bytes 2097152 | tf_op jit(solution)/shard_map/all_to_all | solution.py:170
  4.9 0.7 convert_reduce_fusion
  6.6 30.5 %conditional.1 = (f32[64,128]{1,0:T(8,128)S(1)}, f32[64,128]{1,0:T(8,128)S(1)}, f32[64,128]{1,0:T(8,128)S(1)}, f32[12,128]{1,0:T(8,128)S(1)}, f32[12,128]{1,0:T(...) conditional(s32[]{:T(128)} %convert_element_type.39, ...), branch_computations={%region_1.3_spmd, %region_3.4_spmd} | conditional | flops 38 | bytes 5488942 | solution.py:187
  6.6 0.6 fusion.2
  9.4 1.0 copy.9
  10.3 10.8 %all-to-all-start = ((f32[16,64,128]{2,1,0:T(8,128)}), f32[16,64,128]{2,1,0:T(8,128)S(1)}, u32[]{:S(2)}, u32[]{:S(2)}) async-start(f32[16,64,128]{2,1,0:T(8,128)} %copy.9), calls=%async_computation | async-start | bytes 1048576 | tf_op jit(solution)/shard_map/cond/branch_0_fun/all_to_all | solution.py:177
  21.1 0.7 fusion.15
  27.6 9.5 %all-to-all-done = f32[16,64,128]{2,1,0:T(8,128)S(1)} async-done(((f32[16,64,128]{2,1,0:T(8,128)}), f32[16,64,128]{2,1,0:T(8,128)S(1)}, u32[]{:S(2)}, u32[]{:S(2)}) %all-to-all-start) | async-done | bytes 524320 | tf_op jit(solution)/shard_map/cond/branch_0_fun/all_to_all | solution.py:177
  37.2 4.7 %collective-permute-start = (f32[24,128]{1,0:T(8,128)S(1)}, f32[24,128]{1,0:T(8,128)S(1)}, u32[]{:S(2)}, u32[]{:S(2)}) collective-permute-start(f32[24,128]{1,0:T(8,128)S(1)} %pad_maximum_fusion.4), channel_id=1, source_target_pairs={{0,1},{1,2},{2,3},{3,4},{4,5},{5,6},{6,7},{7,8},{8,9},{9,10},{10,1... | collective-permute-start | bytes 36872 | tf_op jit(solution)/shard_map/ppermute | solution.py:202
  41.9 2.1 %collective-permute-start.1 = (f32[24,128]{1,0:T(8,128)S(1)}, f32[24,128]{1,0:T(8,128)S(1)}, u32[]{:S(2)}, u32[]{:S(2)}) collective-permute-start(f32[24,128]{1,0:T(8,128)S(1)} %pad_maximum_fusion.5), channel_id=1, source_target_pairs={{1,0},{2,1},{3,2},{4,3},{5,4},{6,5},{7,6},{8,7},{9,8},{10,9},{11,1... | collective-permute-start | bytes 36872 | tf_op jit(solution)/shard_map/ppermute | solution.py:203
  44.1 5.9 %collective-permute-done.1 = f32[24,128]{1,0:T(8,128)S(1)} collective-permute-done((f32[24,128]{1,0:T(8,128)S(1)}, f32[24,128]{1,0:T(8,128)S(1)}, u32[]{:S(2)}, u32[]{:S(2)}) %collective-permute-start.1) | collective-permute-done | bytes 12320 | tf_op jit(solution)/shard_map/ppermute | solution.py:203
  50.3 22.1 %all_to_all.23.refs_3_.refs_2_ = f32[8,168,128]{2,1,0:T(8,128)S(1)} all-to-all(f32[8,168,128]{2,1,0:T(8,128)S(1)} %broadcast_in_dim.32), channel_id=1, replica_groups={{0,64,128,192,256,320,384,448},{16,80,144,208,272,336,400,464},{32,96,1..., dimensions={0} | all-to-all | bytes 1376256 | tf_op jit(solution)/shard_map/all_to_all | solution.py:218
  72.4 2.8 %collective-permute-start.2 = (f32[8,168,128]{2,1,0:T(8,128)S(1)}, f32[8,168,128]{2,1,0:T(8,128)S(1)}, u32[]{:S(2)}, u32[]{:S(2)}) collective-permute-start(f32[8,168,128]{2,1,0:T(8,128)S(1)} %all_to_all.23.refs_3_.refs_2_), channel_id=1, source_target_pairs={{0,32},{16,48},{32,0},{48,16},{64,96},{80,112},{96,64},{112,80},{1... | collective-permute-start | bytes 2064392 | tf_op jit(solution)/shard_map/ppermute | solution.py:225
  75.2 12.3 %all_to_all.24.refs_2_ = f32[8,72,128]{2,1,0:T(8,128)S(1)} all-to-all(f32[8,72,128]{2,1,0:T(8,128)S(1)} %broadcast_in_dim.33), channel_id=1, replica_groups={{0,64,128,192,256,320,384,448},{16,80,144,208,272,336,400,464},{32,96,1..., dimensions={0} | all-to-all | bytes 589824 | tf_op jit(solution)/shard_map/all_to_all | solution.py:218
  87.5 1.2 %pad_maximum_fusion = f32[2,8,168,128]{3,2,1,0:T(8,128)} fusion(f32[1,8,168,128]{3,2,1,0:T(8,128)S(1)} %bitcast.67, f32[1,8,168,128]{3,2,1,0:T(8,128)S(1)} %bitcast.66), kind=kLoop, calls=%fused_computation.27 | loop fusion | flops 344064 | bytes 2752512 | tf_op jit(solution)/shard_map/stack | solution.py:221
  88.7 7.1 %collective-permute-start.4 = (f32[2,8,168,128]{3,2,1,0:T(8,128)}, f32[2,8,168,128]{3,2,1,0:T(8,128)S(1)}, u32[]{:S(2)}, u32[]{:S(2)}) collective-permute-start(f32[2,8,168,128]{3,2,1,0:T(8,128)} %pad_maximum_fusion), channel_id=1, source_target_pairs={{0,16},{16,0},{32,48},{48,32},{64,80},{80,64},{96,112},{112,96},{1... | collective-permute-start | bytes 4128776 | tf_op jit(solution)/shard_map/ppermute | solution.py:221
  95.9 2.5 %collective-permute-start.3 = (f32[8,72,128]{2,1,0:T(8,128)S(1)}, f32[8,72,128]{2,1,0:T(8,128)S(1)}, u32[]{:S(2)}, u32[]{:S(2)}) collective-permute-start(f32[8,72,128]{2,1,0:T(8,128)S(1)} %all_to_all.24.refs_2_), channel_id=1, source_target_pairs={{0,32},{16,48},{32,0},{48,16},{64,96},{80,112},{96,64},{112,80},{1... | collective-permute-start | bytes 884744 | tf_op jit(solution)/shard_map/ppermute | solution.py:228
  99.0 0.7 fusion.13
  99.7 0.9 fusion.8
  100.8 4.4 %shard_map.50.refs_1_ = f32[2,112,2048]{2,1,0:T(8,128)S(1)} custom-call(s32[4]{0:T(128)S(1)} %pad_add_fusion.refs_0_, f32[2,112,128]{2,1,0:T(8,128)S(1)} %broadcast_in_dim.36.refs_1_, f32[2,8,2048]{2,1,0:T(8,128)S(1)} %broadcast_in_dim.37.refs_2_, f32[8,168,128]{2,1,0:T(8,128)S(1)} %all_to_all.23.refs_3_.refs_2_, ...), custom_call_target="tpu_custom_call" | custom-call | flops 20000000 | bytes 6000000 | tf_op jit(solution)/shard_map/pallas_call | solution.py:239
  105.2 3.7 %shard_map.51.refs_1_ = f32[2,112,2048]{2,1,0:T(8,128)S(1)} custom-call(s32[4]{0:T(128)S(1)} %pad_add_fusion.refs_0_, f32[2,112,2048]{2,1,0:T(8,128)S(1)} %shard_map.50.refs_1_, f32[8,168,128]{2,1,0:T(8,128)S(1)} %all_to_all.23.refs_3_.refs_2_, f32[8,168,128]{2,1,0:T(8,128)S(1)} %collective-permute-done.2.refs_4_.refs_3_, ...), custom_call_target="tpu_custom_call" | custom-call | flops 20000000 | bytes 6000000 | tf_op jit(solution)/shard_map/pallas_call | solution.py:239
  109.0 2.2 %collective-permute-start.5 = (f32[2,8,72,128]{3,2,1,0:T(8,128)S(1)}, f32[2,8,72,128]{3,2,1,0:T(8,128)S(1)}, u32[]{:S(2)}, u32[]{:S(2)}) collective-permute-start(f32[2,8,72,128]{3,2,1,0:T(8,128)S(1)} %pad_maximum_fusion.1), channel_id=1, source_target_pairs={{0,16},{16,0},{32,48},{48,32},{64,80},{80,64},{96,112},{112,96},{1... | collective-permute-start | bytes 1769480 | tf_op jit(solution)/shard_map/ppermute | solution.py:221
  111.2 1.7 %collective-permute-done.5.refs_4_ = f32[2,8,72,128]{3,2,1,0:T(8,128)S(1)} collective-permute-done((f32[2,8,72,128]{3,2,1,0:T(8,128)S(1)}, f32[2,8,72,128]{3,2,1,0:T(8,128)S(1)}, u32[]{:S(2)}, u32[]{:S(2)}) %collective-permute-start.5) | collective-permute-done | bytes 589856 | tf_op jit(solution)/shard_map/ppermute | solution.py:221
  112.9 4.5 %shard_map.52 = (f32[1,64,2048]{2,1,0:T(8,128)}, f32[1,64,2048]{2,1,0:T(8,128)}) custom-call(s32[4]{0:T(128)S(1)} %pad_add_fusion.refs_0_, f32[2,112,2048]{2,1,0:T(8,128)S(1)} %shard_map.51.refs_1_, f32[8,72,128]{2,1,0:T(8,128)S(1)} %all_to_all.24.refs_2_, f32[8,72,128]{2,1,0:T(8,128)S(1)} %collective-permute-done.3.refs_3_, ...), custom_call_target="tpu_custom_call" | custom-call | flops 20000000 | bytes 6000000 | tf_op jit(solution)/shard_map/pallas_call | solution.py:239
  (36 shorter events, 1.8 us)
Async XLA Ops:
  0.6 4.3 %copy-start = (s32[3]{0:T(128)S(1)}, s32[3]{0:T(128)}, u32[]{:S(2)}) copy-start(s32[3]{0:T(128)} %param.6) | copy-start | bytes 40
  0.6 6.0 %all-to-all-start.2 = ((f32[2,64,2048]{2,1,0:T(8,128)}), f32[2,64,2048]{2,1,0:T(8,128)S(1)}, u32[]{:S(2)}, u32[]{:S(2)}) async-start(f32[2,64,2048]{2,1,0:T(8,128)} %bitcast.75), calls=%async_computation.2 | async-start | bytes 2097152 | tf_op jit(solution)/shard_map/all_to_all | solution.py:170
  10.3 26.8 %all-to-all-start = ((f32[16,64,128]{2,1,0:T(8,128)}), f32[16,64,128]{2,1,0:T(8,128)S(1)}, u32[]{:S(2)}, u32[]{:S(2)}) async-start(f32[16,64,128]{2,1,0:T(8,128)} %copy.9), calls=%async_computation | async-start | bytes 1048576 | tf_op jit(solution)/shard_map/cond/branch_0_fun/all_to_all | solution.py:177
  37.2 6.8 %collective-permute-start = (f32[24,128]{1,0:T(8,128)S(1)}, f32[24,128]{1,0:T(8,128)S(1)}, u32[]{:S(2)}, u32[]{:S(2)}) collective-permute-start(f32[24,128]{1,0:T(8,128)S(1)} %pad_maximum_fusion.4), channel_id=1, source_target_pairs={{0,1},{1,2},{2,3},{3,4},{4,5},{5,6},{6,7},{7,8},{8,9},{9,10},{10,1... | collective-permute-start | bytes 36872 | tf_op jit(solution)/shard_map/ppermute | solution.py:202
  41.9 8.1 %collective-permute-start.1 = (f32[24,128]{1,0:T(8,128)S(1)}, f32[24,128]{1,0:T(8,128)S(1)}, u32[]{:S(2)}, u32[]{:S(2)}) collective-permute-start(f32[24,128]{1,0:T(8,128)S(1)} %pad_maximum_fusion.5), channel_id=1, source_target_pairs={{1,0},{2,1},{3,2},{4,3},{5,4},{6,5},{7,6},{8,7},{9,8},{10,9},{11,1... | collective-permute-start | bytes 36872 | tf_op jit(solution)/shard_map/ppermute | solution.py:203
  72.4 15.1 %collective-permute-start.2 = (f32[8,168,128]{2,1,0:T(8,128)S(1)}, f32[8,168,128]{2,1,0:T(8,128)S(1)}, u32[]{:S(2)}, u32[]{:S(2)}) collective-permute-start(f32[8,168,128]{2,1,0:T(8,128)S(1)} %all_to_all.23.refs_3_.refs_2_), channel_id=1, source_target_pairs={{0,32},{16,48},{32,0},{48,16},{64,96},{80,112},{96,64},{112,80},{1... | collective-permute-start | bytes 2064392 | tf_op jit(solution)/shard_map/ppermute | solution.py:225
  87.5 10.9 %copy-start.1 = (s32[1,2]{1,0:T(1,128)S(1)}, s32[1,2]{1,0:T(1,128)}, u32[]{:S(2)}) copy-start(s32[1,2]{1,0:T(1,128)} %param.7) | copy-start | bytes 28
  88.7 12.0 %collective-permute-start.4 = (f32[2,8,168,128]{3,2,1,0:T(8,128)}, f32[2,8,168,128]{3,2,1,0:T(8,128)S(1)}, u32[]{:S(2)}, u32[]{:S(2)}) collective-permute-start(f32[2,8,168,128]{3,2,1,0:T(8,128)} %pad_maximum_fusion), channel_id=1, source_target_pairs={{0,16},{16,0},{32,48},{48,32},{64,80},{80,64},{96,112},{112,96},{1... | collective-permute-start | bytes 4128776 | tf_op jit(solution)/shard_map/ppermute | solution.py:221
  95.9 13.0 %collective-permute-start.3 = (f32[8,72,128]{2,1,0:T(8,128)S(1)}, f32[8,72,128]{2,1,0:T(8,128)S(1)}, u32[]{:S(2)}, u32[]{:S(2)}) collective-permute-start(f32[8,72,128]{2,1,0:T(8,128)S(1)} %all_to_all.24.refs_2_), channel_id=1, source_target_pairs={{0,32},{16,48},{32,0},{48,16},{64,96},{80,112},{96,64},{112,80},{1... | collective-permute-start | bytes 884744 | tf_op jit(solution)/shard_map/ppermute | solution.py:228
  109.0 3.9 %collective-permute-start.5 = (f32[2,8,72,128]{3,2,1,0:T(8,128)S(1)}, f32[2,8,72,128]{3,2,1,0:T(8,128)S(1)}, u32[]{:S(2)}, u32[]{:S(2)}) collective-permute-start(f32[2,8,72,128]{3,2,1,0:T(8,128)S(1)} %pad_maximum_fusion.1), channel_id=1, source_target_pairs={{0,16},{16,0},{32,48},{48,32},{64,80},{80,64},{96,112},{112,96},{1... | collective-permute-start | bytes 1769480 | tf_op jit(solution)/shard_map/ppermute | solution.py:221

commit v3 on v2

--- a/solution.py
+++ b/solution.py
@@ -46,15 +46,29 @@
     return here, [s + p * h for s, p, h in zip(around, plane, here)]
 
 
-def assemble(place, refs, planes, slab, skip, cols):
-    count, to = 64 + 2 * HALO[slab], TOP - HALO[slab]
-    for ref, core, half in refs:
-        plane = place[1] if core == 0 else 1 - place[1]
-        column = place[0] if half == 0 else 1 - place[0]
+def assemble(place, own, others, planes, slab, skip, cols):
+    halo = HALO[slab]
+    half = 32
+
+    def put(ref, core):
         for z in range(cols // 2):
-            at = pl.ds(pl.multiple_of((2 * z + column) * LANES, LANES), LANES)
-            values = ref[z, skip : skip + count, :]
-            planes[plane, to : to + count, at] = (phase_gain / diffraction) * values - 4.0
+            for q in range(2):
+                column = place[0] if q == 0 else 1 - place[0]
+                at = pl.ds(pl.multiple_of((2 * z + column) * LANES, LANES), LANES)
+                for j in range(2):
+                    for first, count, to in (
+                        (skip + half * j, half, TOP + half * core),
+                        (skip + 2 * half + halo * j, halo, TOP + 2 * half if core else TOP - halo),
+                    ):
+                        values = ref[q][z, first : first + count, :]
+                        planes[j, to : to + count, at] = (phase_gain / diffraction) * values - 4.0
+
+    for core in range(2):
+
+        @pl.when(place[1] == core)
+        def _():
+            put(own, core)
+            put(others, 1 - core)
 
 
 def clear_outside(place, parts):
@@ -128,8 +142,7 @@
     before = None if first else refs.pop(0)
     mine, other, theirs = refs[:3]
     planes, trial, field = refs[-3:]
-    pieces = ((mine, 0, 0), (other, 0, 1), (theirs.at[0], 1, 0), (theirs.at[1], 1, 1))
-    assemble(place, pieces, planes, slab, skip, cols)
+    assemble(place, (mine, other), (theirs.at[0], theirs.at[1]), planes, slab, skip, cols)
     if first:
         incident(*waves, field, cols)
         before = field
@@ -161,29 +174,34 @@
 
 
 def keep(contrast, owners):
-    rows, cols = contrast.shape[1:]
+    depth, rows, cols = contrast.shape
     angs = lax.axis_size("ang")
     chips = angs // 2
     chip = lax.axis_index("ang") // 2
     by_chip = [[2 * i + c for i in range(chips)] for c in range(2)]
     by_core = [[2 * i, 2 * i + 1] for i in range(chips)]
-    planes = lax.all_to_all(contrast, "ang", 0, 0, tiled=True, axis_index_groups=by_core)
+    halves = contrast.reshape(depth, 2, rows // 2, cols).transpose(1, 0, 2, 3).reshape(2, rows, cols)
+    halves = lax.all_to_all(halves, "ang", 0, 0, tiled=True, axis_index_groups=by_core)
     owner_chip, owner_core = owners // 2, owners % 2
+    core = jnp.sum(jnp.where(owner_chip == chip, owner_core, 0))
+    shared = (owner_chip[:, None] == owner_chip[None, :]).sum() > owners.shape[0]
+    halves, core, shared = lax.optimization_barrier((halves, core, shared))
+
+    def at(tiles, i):
+        return lax.dynamic_index_in_dim(tiles, i, 0, keepdims=False, allow_negative_indices=False)
 
     def one():
-        core = jnp.sum(jnp.where(owner_chip == chip, owner_core, 0))
-        plane = lax.dynamic_index_in_dim(planes, core, 0, keepdims=False)
-        tiles = plane.reshape(rows, chips, cols // chips).transpose(1, 0, 2)
+        half = jnp.where(core == 1, halves[1], halves[0])
+        tiles = half.reshape(rows, chips, cols // chips).transpose(1, 0, 2)
         tiles = lax.all_to_all(tiles, "ang", 0, 0, tiled=True, axis_index_groups=by_chip)
-        return tuple(lax.dynamic_index_in_dim(tiles, c, 0, keepdims=False) for c in owner_chip)
+        return tuple(at(tiles, c) for c in owner_chip)
 
     def both():
-        tiles = planes.reshape(2, rows, chips, cols // chips).transpose(2, 0, 1, 3)
+        tiles = halves.reshape(2, rows, chips, cols // chips).transpose(2, 0, 1, 3)
         tiles = lax.all_to_all(tiles, "ang", 0, 0, tiled=True, axis_index_groups=by_chip)
         tiles = tiles.reshape(angs, rows, cols // chips)
-        return tuple(lax.dynamic_index_in_dim(tiles, o, 0, keepdims=False) for o in owners)
-
-    shared = (owner_chip[:, None] == owner_chip[None, :]).sum() > owners.shape[0]
+        return tuple(at(tiles, o) for o in owners)
+
     return lax.cond(shared, both, one)
 
 
@@ -197,10 +215,16 @@
 
     kept = keep(contrast[0], owners)
 
-    tails = jnp.concatenate([kept[k][rows - HALO[k] :] for k in range(slabs)], axis=0)
-    heads = jnp.concatenate([kept[k][: HALO[k]] for k in range(slabs)], axis=0)
-    above = lax.ppermute(tails, "xy", [(i, i + 1) for i in range(spots - 1)])
-    below = lax.ppermute(heads, "xy", [(i + 1, i) for i in range(spots - 1)])
+    half = rows // 2
+    heads = [kept[k][half * j : half * j + HALO[k]] for k in range(slabs) for j in range(depth)]
+    tails = [kept[k][half * (j + 1) - HALO[k] : half * (j + 1)] for k in range(slabs) for j in range(depth)]
+    edge = jnp.where(ang % 2 == 0, jnp.concatenate(heads, axis=0), jnp.concatenate(tails, axis=0))
+    up = [(spots * a + i, spots * (a + 1) + i - 1) for a in range(0, angs, 2) for i in range(1, spots)]
+    edge = lax.ppermute(edge, ("ang", "xy"), up + [(j, i) for i, j in up])
+
+    tilts, kept = lax.optimization_barrier((tilts, kept))
+    wave = waves(tilts, spot * rows, rows * spots, cols)
+    edge, wave = lax.optimization_barrier((edge, wave))
 
     columns = [[4 * z + q for z in range(angs // 4)] for q in range(4)]
     swap_x = [(i, i ^ 2) for i in range(angs)]
@@ -209,8 +233,7 @@
     def along_z(chosen, after=None):
         parts = []
         for k in chosen:
-            at = slice(sum(HALO[:k]), sum(HALO[: k + 1]))
-            parts += [above[at], kept[k], below[at]]
+            parts += [kept[k], edge[depth * sum(HALO[:k]) : depth * sum(HALO[: k + 1])]]
         piece = jnp.concatenate(parts, axis=0)
         if after is not None:
             piece, after = lax.optimization_barrier((piece, after))
@@ -224,11 +247,10 @@
     mine = along_z(early)
     other = lax.ppermute(mine, "ang", swap_x)
     late_mine = along_z(late, mine)
-    late_mine, other, tilts = lax.optimization_barrier((late_mine, other, tilts))
+    late_mine, other = lax.optimization_barrier((late_mine, other))
     late_other = lax.ppermute(late_mine, "ang", swap_x)
     first = mine, other, from_core(mine, other)
 
-    wave = waves(tilts, spot * rows, rows * spots, cols)
     place = jnp.stack([ang // 2 % 2, ang % 2, spot, jnp.int32(spots - 1)])
 
     def step(slab, before, pieces):

time: 118 us -> 119 us (level)
  loops' own time: 7.8 us -> 0.69 us
  local copies, waits for them, and re-layouts: 2.85 us -> 8.51 us
  starting transfers between devices: 36.3 us -> 32 us
  blocking collectives: 34.4 us -> 38.6 us
  waiting for transfers between devices: 17.5 us -> 19.7 us
    another operation x1, loops' own time: 7.8 us -> 0.69 us  [keep(): return lax.cond(shared, both, one)]
    all_to_all x1, waiting for transfers between devices: 9.53 us -> 15.6 us  [one(): lax.all_to_all(tiles, 'ang', 0, 0, tiled=True, axis_index_groups=by_chip)]
    ppermute x2 -> x1, waiting for transfers between devices: 5.88 us -> 0.01 us  [per_device(): edge = lax.ppermute(edge, ('ang', 'xy'), up + [(j, i) for i, j in up])]
    all_to_all x2, blocking collectives: 34.4 us -> 38.6 us  [along_z(): lax.all_to_all(copies, 'ang', 0, 0, tiled=True, axis_index_groups=columns)]
    ppermute x2, starting transfers between devices: 9.27 us -> 5.4 us  [from_core(): return lax.ppermute(jnp.stack([mine, other]), 'ang', swap_core)]
    another operation x1 -> x2, local copies, waits for them, and re-layouts: 0.67 us -> 2.97 us  [the longest x1 2.33 us: keep(): contrast.reshape(depth, 2, rows // 2, cols).transpose(1, 0, 2, 3)]
    squeeze x1, local copies, waits for them, and re-layouts: 0.01 us -> 1.88 us  [at(): lax.dynamic_index_in_dim(tiles, i, 0, keepdims=False, allow_negative_indi...]
    ppermute x1, waiting for transfers between devices: 0.01 us -> 1.79 us  [per_device(): other = lax.ppermute(mine, 'ang', swap_x)]
  transfers between devices with their start and end apart: 8 -> 7, of which waited for: 4 -> 4; matrix products, arithmetic and copies ran while one was open for 3% -> 4% of each run, Pallas kernels for 7% -> 7%
where the time goes in v3:
time: 119 us; the launch traced here: 118 us
  blocking collectives  38.6 us (32%)
  starting transfers between devices  32 us (27%)
  waiting for transfers between devices  19.7 us (17%)
  Pallas kernels  12.9 us (11%)
  local copies, waits for them, and re-layouts  8.51 us (7%)
  other arithmetic  4.35 us (4%)
  between operations  1.53 us (1%)
    all_to_all x2, blocking collectives, along_z(): lax.all_to_all(copies, 'ang', 0, 0, tiled=True, axis_index_groups=columns)  38.6 us
    all_to_all x1, waiting for transfers between devices, one(): lax.all_to_all(tiles, 'ang', 0, 0, tiled=True, axis_index_groups=by_chip)  15.6 us
    pallas_call x3, Pallas kernels, step(): pl.pallas_call(functools.partial(through, slab=slab, skip=sum((rows + 2 *...  12.9 us
    all_to_all x1, starting transfers between devices, one(): lax.all_to_all(tiles, 'ang', 0, 0, tiled=True, axis_index_groups=by_chip)  10.8 us
    ppermute x1, starting transfers between devices, per_device(): edge = lax.ppermute(edge, ('ang', 'xy'), up + [(j, i) for i, j in up])  7.08 us
    ppermute x2, starting transfers between devices, from_core(): return lax.ppermute(jnp.stack([mine, other]), 'ang', swap_core)  5.4 us
    all_to_all x1, starting transfers between devices, keep(): lax.all_to_all(halves, 'ang', 0, 0, tiled=True, axis_index_groups=by_core)  4.37 us
  transfers between devices with their start and end apart: 7, of which 4 were waited for; matrix products, arithmetic and copies ran while one was open for 4% of the time, Pallas kernels for 7%

profile of v3, /device:TPU:29, one launch (start us, length us, event | category | flops | bytes accessed | tf_op | source)
XLA Modules:
  0.0 118.3 jit_solution(6349389318117223383)
XLA Ops:
  0.6 2.3 %copy.15 = f32[2,2,32,2048]{3,2,0,1:T(8,128)} copy(f32[2,2,32,2048]{3,2,1,0:T(8,128)} %bitcast.55) | data formatting | bytes 2097152 | tf_op jit(solution)/shard_map/reshape;squeeze | solution.py:183
  3.0 4.4 %all-to-all-start.2 = ((f32[2,64,2048]{2,1,0:T(8,128)}), f32[2,64,2048]{2,1,0:T(8,128)S(1)}, u32[]{:S(2)}, u32[]{:S(2)}) async-start(f32[2,64,2048]{2,1,0:T(8,128)} %bitcast.20), calls=%async_computation.2 | async-start | bytes 2097152 | tf_op jit(solution)/shard_map/all_to_all | solution.py:184
  8.0 0.7 convert_reduce_fusion
  9.3 30.8 %conditional.1 = (f32[64,128]{1,0:T(8,128)S(1)}, f32[64,128]{1,0:T(8,128)S(1)}, f32[64,128]{1,0:T(8,128)S(1)}) conditional(s32[]{:T(128)} %convert_element_type.39, (s32[]{:T(128)}, f32[2,64,2048]{2,1,0:T(8,128)S(1)}, s32[3]{0:T(128)S(1)}) %tuple.22, (f32[2,64,2048]{2,1,0:T(8,128)S(1)}, s32[3]{0:T(128)S(1)}) %tuple.52), branch_computations={%region_2.3_spmd, %region_3.4_spmd} | conditional | flops 131073 | bytes 9633884 | solution.py:205
  10.2 1.0 copy.19
  11.1 10.8 %all-to-all-start = ((f32[16,64,128]{2,1,0:T(8,128)}), f32[16,64,128]{2,1,0:T(8,128)S(1)}, u32[]{:S(2)}, u32[]{:S(2)}) async-start(f32[16,64,128]{2,1,0:T(8,128)} %bitcast.45), calls=%async_computation | async-start | bytes 1048576 | tf_op jit(solution)/shard_map/cond/branch_0_fun/all_to_all | solution.py:196
  22.6 15.6 %all-to-all-done = f32[16,64,128]{2,1,0:T(8,128)S(1)} async-done(((f32[16,64,128]{2,1,0:T(8,128)}), f32[16,64,128]{2,1,0:T(8,128)S(1)}, u32[]{:S(2)}, u32[]{:S(2)}) %all-to-all-start) | async-done | bytes 524320 | tf_op jit(solution)/shard_map/cond/branch_0_fun/all_to_all | solution.py:196
  38.2 1.9 %dynamic-slice_bitcast_fusion = (f32[64,128]{1,0:T(8,128)S(1)}, f32[64,128]{1,0:T(8,128)S(1)}, f32[64,128]{1,0:T(8,128)S(1)}) fusion(f32[16,64,128]{2,1,0:T(8,128)S(1)} %all-to-all-done, s32[]{:T(128)} %bitcast.5, s32[]{:T(128)} %bitcast.3, s32[]{:T(128)} %bitcast.1), kind=kLoop, calls=%fused_computation.2 | loop fusion | bytes 196620 | tf_op jit(solution)/shard_map/cond/branch_0_fun/jit(dynamic_index_in_dim)/squeeze | solution.py:191
  40.5 7.1 %collective-permute-start = (f32[48,128]{1,0:T(8,128)S(1)}, f32[48,128]{1,0:T(8,128)S(1)}, u32[]{:S(2)}, u32[]{:S(2)}) collective-permute-start(f32[48,128]{1,0:T(8,128)S(1)} %broadcast_select_fusion), channel_id=1, source_target_pairs={{1,16},{2,17},{3,18},{4,19},{5,20},{6,21},{7,22},{8,23},{9,24},{10... | collective-permute-start | bytes 73736 | tf_op jit(solution)/shard_map/ppermute | solution.py:223
  48.1 0.9 fusion.3
  49.8 0.7 broadcast_in_dim.32.refs_1_
  50.6 24.1 %all_to_all.23.refs_3_.refs_2_ = f32[8,168,128]{2,1,0:T(8,128)S(1)} all-to-all(f32[8,168,128]{2,1,0:T(8,128)S(1)} %broadcast_in_dim.34), channel_id=1, replica_groups={{0,64,128,192,256,320,384,448},{16,80,144,208,272,336,400,464},{32,96,1..., dimensions={0} | all-to-all | bytes 1376256 | tf_op jit(solution)/shard_map/all_to_all | solution.py:241
  74.7 2.2 %collective-permute-start.1 = (f32[8,168,128]{2,1,0:T(8,128)S(1)}, f32[8,168,128]{2,1,0:T(8,128)S(1)}, u32[]{:S(2)}, u32[]{:S(2)}) collective-permute-start(f32[8,168,128]{2,1,0:T(8,128)S(1)} %all_to_all.23.refs_3_.refs_2_), channel_id=1, source_target_pairs={{0,32},{16,48},{32,0},{48,16},{64,96},{80,112},{96,64},{112,80},{1... | collective-permute-start | bytes 2064392 | tf_op jit(solution)/shard_map/ppermute | solution.py:248
  77.0 14.5 %all_to_all.24.refs_2_ = f32[8,72,128]{2,1,0:T(8,128)S(1)} all-to-all(f32[8,72,128]{2,1,0:T(8,128)S(1)} %broadcast_in_dim.35), channel_id=1, replica_groups={{0,64,128,192,256,320,384,448},{16,80,144,208,272,336,400,464},{32,96,1..., dimensions={0} | all-to-all | bytes 589824 | tf_op jit(solution)/shard_map/all_to_all | solution.py:241
  91.5 1.8 %collective-permute-done.1.refs_4_.refs_3_ = f32[8,168,128]{2,1,0:T(8,128)S(1)} collective-permute-done((f32[8,168,128]{2,1,0:T(8,128)S(1)}, f32[8,168,128]{2,1,0:T(8,128)S(1)}, u32[]{:S(2)}, u32[]{:S(2)}) %collective-permute-start.1) | collective-permute-done | bytes 688160 | tf_op jit(solution)/shard_map/ppermute | solution.py:248
  93.2 1.2 pad_maximum_fusion
  94.4 3.1 %collective-permute-start.3 = (f32[2,8,168,128]{3,2,1,0:T(8,128)}, f32[2,8,168,128]{3,2,1,0:T(8,128)S(1)}, u32[]{:S(2)}, u32[]{:S(2)}) collective-permute-start(f32[2,8,168,128]{3,2,1,0:T(8,128)} %pad_maximum_fusion), channel_id=1, source_target_pairs={{0,16},{16,0},{32,48},{48,32},{64,80},{80,64},{96,112},{112,96},{1... | collective-permute-start | bytes 4128776 | tf_op jit(solution)/shard_map/ppermute | solution.py:244
  97.6 2.2 %collective-permute-start.2 = (f32[8,72,128]{2,1,0:T(8,128)S(1)}, f32[8,72,128]{2,1,0:T(8,128)S(1)}, u32[]{:S(2)}, u32[]{:S(2)}) collective-permute-start(f32[8,72,128]{2,1,0:T(8,128)S(1)} %all_to_all.24.refs_2_), channel_id=1, source_target_pairs={{0,32},{16,48},{32,0},{48,16},{64,96},{80,112},{96,64},{112,80},{1... | collective-permute-start | bytes 884744 | tf_op jit(solution)/shard_map/ppermute | solution.py:251
  100.5 0.9 copy-done
  101.4 4.4 %shard_map.50.refs_1_ = f32[2,112,2048]{2,1,0:T(8,128)S(1)} custom-call(s32[4]{0:T(128)S(1)} %pad_add_fusion.refs_0_, f32[2,112,128]{2,1,0:T(8,128)S(1)} %copy-done, f32[2,8,2048]{2,1,0:T(8,128)S(1)} %broadcast_in_dim.33.refs_2_, f32[8,168,128]{2,1,0:T(8,128)S(1)} %all_to_all.23.refs_3_.refs_2_, f32[8,168,128]{2,1,0:T(8,128)S(1)} %collective-permute-done.1.refs_4_.refs_3_, ...), custom_call_target="tpu_custom_call" | custom-call | flops 20000000 | bytes 6000000 | tf_op jit(solution)/shard_map/pallas_call | solution.py:261
  105.8 3.8 %shard_map.51.refs_1_ = f32[2,112,2048]{2,1,0:T(8,128)S(1)} custom-call(s32[4]{0:T(128)S(1)} %pad_add_fusion.refs_0_, f32[2,112,2048]{2,1,0:T(8,128)S(1)} %shard_map.50.refs_1_, f32[8,168,128]{2,1,0:T(8,128)S(1)} %all_to_all.23.refs_3_.refs_2_, f32[8,168,128]{2,1,0:T(8,128)S(1)} %collective-permute-done.1.refs_4_.refs_3_, ...), custom_call_target="tpu_custom_call" | custom-call | flops 20000000 | bytes 6000000 | tf_op jit(solution)/shard_map/pallas_call | solution.py:261
  109.6 2.3 %collective-permute-start.4 = (f32[2,8,72,128]{3,2,1,0:T(8,128)S(1)}, f32[2,8,72,128]{3,2,1,0:T(8,128)S(1)}, u32[]{:S(2)}, u32[]{:S(2)}) collective-permute-start(f32[2,8,72,128]{3,2,1,0:T(8,128)S(1)} %pad_maximum_fusion.1), channel_id=1, source_target_pairs={{0,16},{16,0},{32,48},{48,32},{64,80},{80,64},{96,112},{112,96},{1... | collective-permute-start | bytes 1769480 | tf_op jit(solution)/shard_map/ppermute | solution.py:244
  111.9 1.6 %collective-permute-done.4.refs_4_ = f32[2,8,72,128]{3,2,1,0:T(8,128)S(1)} collective-permute-done((f32[2,8,72,128]{3,2,1,0:T(8,128)S(1)}, f32[2,8,72,128]{3,2,1,0:T(8,128)S(1)}, u32[]{:S(2)}, u32[]{:S(2)}) %collective-permute-start.4) | collective-permute-done | bytes 589856 | tf_op jit(solution)/shard_map/ppermute | solution.py:244
  113.5 4.7 %shard_map.52 = (f32[1,64,2048]{2,1,0:T(8,128)}, f32[1,64,2048]{2,1,0:T(8,128)}) custom-call(s32[4]{0:T(128)S(1)} %pad_add_fusion.refs_0_, f32[2,112,2048]{2,1,0:T(8,128)S(1)} %shard_map.51.refs_1_, f32[8,72,128]{2,1,0:T(8,128)S(1)} %all_to_all.24.refs_2_, f32[8,72,128]{2,1,0:T(8,128)S(1)} %collective-permute-done.2.refs_3_, ...), custom_call_target="tpu_custom_call" | custom-call | flops 20000000 | bytes 6000000 | tf_op jit(solution)/shard_map/pallas_call | solution.py:261
  (34 shorter events, 3.9 us)
Async XLA Ops:
  3.0 4.4 %copy-start.1 = (s32[3]{0:T(128)S(1)}, s32[3]{0:T(128)}, u32[]{:S(2)}) copy-start(s32[3]{0:T(128)} %param.6) | copy-start | bytes 40
  3.0 6.4 %all-to-all-start.2 = ((f32[2,64,2048]{2,1,0:T(8,128)}), f32[2,64,2048]{2,1,0:T(8,128)S(1)}, u32[]{:S(2)}, u32[]{:S(2)}) async-start(f32[2,64,2048]{2,1,0:T(8,128)} %bitcast.20), calls=%async_computation.2 | async-start | bytes 2097152 | tf_op jit(solution)/shard_map/all_to_all | solution.py:184
  9.3 38.2 %copy-start.2 = (s32[1,2]{1,0:T(1,128)S(1)}, s32[1,2]{1,0:T(1,128)}, u32[]{:S(2)}) copy-start(s32[1,2]{1,0:T(1,128)} %param.7) | copy-start | bytes 28
  11.1 27.1 %all-to-all-start = ((f32[16,64,128]{2,1,0:T(8,128)}), f32[16,64,128]{2,1,0:T(8,128)S(1)}, u32[]{:S(2)}, u32[]{:S(2)}) async-start(f32[16,64,128]{2,1,0:T(8,128)} %bitcast.45), calls=%async_computation | async-start | bytes 1048576 | tf_op jit(solution)/shard_map/cond/branch_0_fun/all_to_all | solution.py:196
  40.5 9.3 %collective-permute-start = (f32[48,128]{1,0:T(8,128)S(1)}, f32[48,128]{1,0:T(8,128)S(1)}, u32[]{:S(2)}, u32[]{:S(2)}) collective-permute-start(f32[48,128]{1,0:T(8,128)S(1)} %broadcast_select_fusion), channel_id=1, source_target_pairs={{1,16},{2,17},{3,18},{4,19},{5,20},{6,21},{7,22},{8,23},{9,24},{10... | collective-permute-start | bytes 73736 | tf_op jit(solution)/shard_map/ppermute | solution.py:223
  74.7 18.5 %collective-permute-start.1 = (f32[8,168,128]{2,1,0:T(8,128)S(1)}, f32[8,168,128]{2,1,0:T(8,128)S(1)}, u32[]{:S(2)}, u32[]{:S(2)}) collective-permute-start(f32[8,168,128]{2,1,0:T(8,128)S(1)} %all_to_all.23.refs_3_.refs_2_), channel_id=1, source_target_pairs={{0,32},{16,48},{32,0},{48,16},{64,96},{80,112},{96,64},{112,80},{1... | collective-permute-start | bytes 2064392 | tf_op jit(solution)/shard_map/ppermute | solution.py:248
  94.4 6.1 %collective-permute-start.3 = (f32[2,8,168,128]{3,2,1,0:T(8,128)}, f32[2,8,168,128]{3,2,1,0:T(8,128)S(1)}, u32[]{:S(2)}, u32[]{:S(2)}) collective-permute-start(f32[2,8,168,128]{3,2,1,0:T(8,128)} %pad_maximum_fusion), channel_id=1, source_target_pairs={{0,16},{16,0},{32,48},{48,32},{64,80},{80,64},{96,112},{112,96},{1... | collective-permute-start | bytes 4128776 | tf_op jit(solution)/shard_map/ppermute | solution.py:244
  97.6 12.0 %collective-permute-start.2 = (f32[8,72,128]{2,1,0:T(8,128)S(1)}, f32[8,72,128]{2,1,0:T(8,128)S(1)}, u32[]{:S(2)}, u32[]{:S(2)}) collective-permute-start(f32[8,72,128]{2,1,0:T(8,128)S(1)} %all_to_all.24.refs_2_), channel_id=1, source_target_pairs={{0,32},{16,48},{32,0},{48,16},{64,96},{80,112},{96,64},{112,80},{1... | collective-permute-start | bytes 884744 | tf_op jit(solution)/shard_map/ppermute | solution.py:251
  100.5 0.9 copy-start
  109.6 3.9 %collective-permute-start.4 = (f32[2,8,72,128]{3,2,1,0:T(8,128)S(1)}, f32[2,8,72,128]{3,2,1,0:T(8,128)S(1)}, u32[]{:S(2)}, u32[]{:S(2)}) collective-permute-start(f32[2,8,72,128]{3,2,1,0:T(8,128)S(1)} %pad_maximum_fusion.1), channel_id=1, source_target_pairs={{0,16},{16,0},{32,48},{48,32},{64,80},{80,64},{96,112},{112,96},{1... | collective-permute-start | bytes 1769480 | tf_op jit(solution)/shard_map/ppermute | solution.py:244

commit v4 on v3

--- a/solution.py
+++ b/solution.py
@@ -11,7 +11,7 @@
 diffraction = 0.05
 phase_gain = 0.08
 
-HALO = (12, 8, 4)
+HALO = (11, 9, 7, 5, 3, 1)
 TOP = 24
 ROWS = 112
 LANES = 128
@@ -46,8 +46,7 @@
     return here, [s + p * h for s, p, h in zip(around, plane, here)]
 
 
-def assemble(place, own, others, planes, slab, skip, cols):
-    halo = HALO[slab]
+def assemble(place, own, others, planes, slab, place_in, cols):
     half = 32
 
     def put(ref, core):
@@ -55,13 +54,16 @@
             for q in range(2):
                 column = place[0] if q == 0 else 1 - place[0]
                 at = pl.ds(pl.multiple_of((2 * z + column) * LANES, LANES), LANES)
+                rim = place_in[1]
                 for j in range(2):
+                    halo = HALO[2 * slab + j]
                     for first, count, to in (
-                        (skip + half * j, half, TOP + half * core),
-                        (skip + 2 * half + halo * j, halo, TOP + 2 * half if core else TOP - halo),
+                        (place_in[0] + half * j, half, TOP + half * core),
+                        (rim, halo, TOP + 2 * half if core else TOP - halo),
                     ):
                         values = ref[q][z, first : first + count, :]
                         planes[j, to : to + count, at] = (phase_gain / diffraction) * values - 4.0
+                    rim += halo
 
     for core in range(2):
 
@@ -135,14 +137,14 @@
     lax.fori_loop(0, ROWS // 8, start, 0, unroll=2)
 
 
-def through(*refs, slab, skip, cols, first, last):
+def through(*refs, slab, place_in, cols, first, last):
     refs = list(refs)
     place = refs.pop(0)
     waves = [refs.pop(0) for _ in range(2)] if first else []
     before = None if first else refs.pop(0)
     mine, other, theirs = refs[:3]
     planes, trial, field = refs[-3:]
-    assemble(place, (mine, other), (theirs.at[0], theirs.at[1]), planes, slab, skip, cols)
+    assemble(place, (mine, other), (theirs.at[0], theirs.at[1]), planes, slab, place_in, cols)
     if first:
         incident(*waves, field, cols)
         before = field
@@ -173,34 +175,36 @@
     )
 
 
-def keep(contrast, owners):
+def keep(contrast, owners, wave):
     depth, rows, cols = contrast.shape
     angs = lax.axis_size("ang")
     chips = angs // 2
     chip = lax.axis_index("ang") // 2
     by_chip = [[2 * i + c for i in range(chips)] for c in range(2)]
-    by_core = [[2 * i, 2 * i + 1] for i in range(chips)]
-    halves = contrast.reshape(depth, 2, rows // 2, cols).transpose(1, 0, 2, 3).reshape(2, rows, cols)
-    halves = lax.all_to_all(halves, "ang", 0, 0, tiled=True, axis_index_groups=by_core)
+    first = lax.axis_index("ang") % 2 == 0
+    top, bottom = contrast[:, : rows // 2], contrast[:, rows // 2 :]
+    given = jnp.where(first, bottom, top)
+    got = lax.ppermute(given, "ang", [(i, i ^ 1) for i in range(angs)])
     owner_chip, owner_core = owners // 2, owners % 2
     core = jnp.sum(jnp.where(owner_chip == chip, owner_core, 0))
     shared = (owner_chip[:, None] == owner_chip[None, :]).sum() > owners.shape[0]
-    halves, core, shared = lax.optimization_barrier((halves, core, shared))
-
+    got, core, shared = lax.optimization_barrier((got, core, shared))
     def at(tiles, i):
-        return lax.dynamic_index_in_dim(tiles, i, 0, keepdims=False, allow_negative_indices=False)
+        return lax.dynamic_index_in_dim(tiles, i, 0, keepdims=False)
 
     def one():
-        half = jnp.where(core == 1, halves[1], halves[0])
+        kept = jnp.where(first, top, bottom)
+        half = jnp.where((core == 0) == first, kept, got)
         tiles = half.reshape(rows, chips, cols // chips).transpose(1, 0, 2)
         tiles = lax.all_to_all(tiles, "ang", 0, 0, tiled=True, axis_index_groups=by_chip)
-        return tuple(at(tiles, c) for c in owner_chip)
+        return tuple(at(tiles, c) for c in owner_chip), wave()
 
     def both():
+        halves = jnp.stack([jnp.where(first, top, got), jnp.where(first, got, bottom)])
         tiles = halves.reshape(2, rows, chips, cols // chips).transpose(2, 0, 1, 3)
         tiles = lax.all_to_all(tiles, "ang", 0, 0, tiled=True, axis_index_groups=by_chip)
         tiles = tiles.reshape(angs, rows, cols // chips)
-        return tuple(at(tiles, o) for o in owners)
+        return tuple(at(tiles, o) for o in owners), wave()
 
     return lax.cond(shared, both, one)
 
@@ -213,28 +217,24 @@
     spot = lax.axis_index("xy")
     angs = lax.axis_size("ang")
 
-    kept = keep(contrast[0], owners)
+    kept, wave = keep(contrast[0], owners, lambda: waves(tilts, spot * rows, rows * spots, cols))
 
     half = rows // 2
-    heads = [kept[k][half * j : half * j + HALO[k]] for k in range(slabs) for j in range(depth)]
-    tails = [kept[k][half * (j + 1) - HALO[k] : half * (j + 1)] for k in range(slabs) for j in range(depth)]
+    slices = [(k, j, HALO[depth * k + j]) for k in range(slabs) for j in range(depth)]
+    heads = [kept[k][half * j : half * j + halo] for k, j, halo in slices]
+    tails = [kept[k][half * (j + 1) - halo : half * (j + 1)] for k, j, halo in slices]
     edge = jnp.where(ang % 2 == 0, jnp.concatenate(heads, axis=0), jnp.concatenate(tails, axis=0))
     up = [(spots * a + i, spots * (a + 1) + i - 1) for a in range(0, angs, 2) for i in range(1, spots)]
     edge = lax.ppermute(edge, ("ang", "xy"), up + [(j, i) for i, j in up])
 
-    tilts, kept = lax.optimization_barrier((tilts, kept))
-    wave = waves(tilts, spot * rows, rows * spots, cols)
-    edge, wave = lax.optimization_barrier((edge, wave))
-
     columns = [[4 * z + q for z in range(angs // 4)] for q in range(4)]
     swap_x = [(i, i ^ 2) for i in range(angs)]
     swap_core = [(i, i ^ 1) for i in range(angs)]
 
     def along_z(chosen, after=None):
-        parts = []
-        for k in chosen:
-            parts += [kept[k], edge[depth * sum(HALO[:k]) : depth * sum(HALO[: k + 1])]]
-        piece = jnp.concatenate(parts, axis=0)
+        rims = [edge[sum(HALO[: depth * k]) : sum(HALO[: depth * (k + 1)])] for k in chosen]
+        spare = jnp.zeros((-sum(r.shape[0] for r in rims) % 8, cols // (angs // 2)), jnp.float32)
+        piece = jnp.concatenate([kept[k] for k in chosen] + rims + [spare], axis=0)
         if after is not None:
             piece, after = lax.optimization_barrier((piece, after))
         copies = jnp.broadcast_to(piece, (angs // 4,) + piece.shape)
@@ -255,6 +255,7 @@
 
     def step(slab, before, pieces):
         start, end = slab == 0, slab == slabs - 1
+        chosen = early if slab in early else late
         state = jax.ShapeDtypeStruct((2, ROWS, cols), jnp.float32)
         out = jax.ShapeDtypeStruct((1, rows, cols), jnp.float32)
         in_vmem = pl.BlockSpec(memory_space=pltpu.VMEM)
@@ -262,7 +263,7 @@
             functools.partial(
                 through,
                 slab=slab,
-                skip=sum(rows + 2 * HALO[k] for k in early if k < slab) if slab in early else 0,
+                place_in=(rows * chosen.index(slab), rows * len(chosen) + sum(HALO[depth * chosen[0] : depth * slab])),
                 cols=cols // LANES,
                 first=start,
                 last=end,

time: 119 us -> 113 us (0.950)
  blocking collectives: 38.6 us -> 14.4 us
  waiting for transfers between devices: 19.7 us -> 33 us
  loops' own time: 0.69 us -> 6.71 us
  local copies, waits for them, and re-layouts: 8.51 us -> 3.97 us
  starting transfers between devices: 32 us -> 34.3 us
  other arithmetic: 4.35 us -> 5.86 us
    all_to_all x2 -> x1, blocking collectives: 38.6 us -> 14.4 us  [along_z(): lax.all_to_all(copies, 'ang', 0, 0, tiled=True, axis_index_groups=columns)]
    all_to_all x1, waiting for transfers between devices: 0.01 us -> 20.7 us  [along_z(): lax.all_to_all(copies, 'ang', 0, 0, tiled=True, axis_index_groups=columns)]
    all_to_all x1, waiting for transfers between devices: 15.6 us -> 7.41 us  [one(): lax.all_to_all(tiles, 'ang', 0, 0, tiled=True, axis_index_groups=by_chip)]
    another operation x1, loops' own time: 0.69 us -> 6.71 us  [keep(): return lax.cond(shared, both, one)]
    ppermute x0 -> x1, starting transfers between devices: none -> 2.58 us  [keep(): got = lax.ppermute(given, 'ang', [(i, i ^ 1) for i in range(angs)])]
    another operation x2 -> x1, local copies, waits for them, and re-layouts: 2.97 us -> 0.65 us  [one(): return (tuple((at(tiles, c) for c in owner_chip)), wave())]
    squeeze x1, local copies, waits for them, and re-layouts: 1.88 us -> 0.01 us  [at(): return lax.dynamic_index_in_dim(tiles, i, 0, keepdims=False)]
    ppermute x1, waiting for transfers between devices: 0.01 us -> 1.66 us  [per_device(): edge = lax.ppermute(edge, ('ang', 'xy'), up + [(j, i) for i, j in up])]
  transfers between devices with their start and end apart: 7 -> 8, of which waited for: 4 -> 6; matrix products, arithmetic and copies ran while one was open for 4% -> 4% of each run, Pallas kernels for 7% -> 7%
where the time goes in v4:
time: 113 us
  starting transfers between devices  34.3 us (30%)
  waiting for transfers between devices  33 us (29%)
  blocking collectives  14.4 us (13%)
  Pallas kernels  12.9 us (11%)
  loops' own time  6.71 us (6%)
  other arithmetic  5.86 us (5%)
  local copies, waits for them, and re-layouts  3.97 us (4%)
  between operations  1.5 us (1%)
    all_to_all x1, waiting for transfers between devices, along_z(): lax.all_to_all(copies, 'ang', 0, 0, tiled=True, axis_index_groups=columns)  20.7 us
    all_to_all x1, blocking collectives, along_z(): lax.all_to_all(copies, 'ang', 0, 0, tiled=True, axis_index_groups=columns)  14.4 us
    pallas_call x3, Pallas kernels, step(): pl.pallas_call(functools.partial(through, slab=slab, place_in=(rows * cho...  12.9 us
    all_to_all x1, starting transfers between devices, one(): lax.all_to_all(tiles, 'ang', 0, 0, tiled=True, axis_index_groups=by_chip)  10.8 us
    all_to_all x1, waiting for transfers between devices, one(): lax.all_to_all(tiles, 'ang', 0, 0, tiled=True, axis_index_groups=by_chip)  7.41 us
    ppermute x1, starting transfers between devices, per_device(): edge = lax.ppermute(edge, ('ang', 'xy'), up + [(j, i) for i, j in up])  7.04 us
    another operation x1, loops' own time, keep(): return lax.cond(shared, both, one)  6.71 us
    ppermute x2, starting transfers between devices, from_core(): return lax.ppermute(jnp.stack([mine, other]), 'ang', swap_core)  5.43 us
  transfers between devices with their start and end apart: 8, of which 6 were waited for; matrix products, arithmetic and copies ran while one was open for 4% of the time, Pallas kernels for 7%

profile of v4, /device:TPU:29, one launch (start us, length us, event | category | flops | bytes accessed | tf_op | source)
XLA Modules:
  0.0 112.6 jit_solution(16309284486628786433)
XLA Ops:
  0.7 1.4 %fusion.33 = (f32[2,32,2048]{2,1,0:T(8,128)S(1)}, f32[2,32,2048]{2,1,0:T(8,128)S(1)}, f32[2,32,2048]{2,1,0:T(8,128)S(1)}) fusion(f32[2,64,2048]{2,1,0:T(8,128)} %bitcast.111, pred[]{:T(512)} %eq.42), kind=kLoop, calls=%fused_computation.99 | loop fusion | flops 131072 | bytes 2621441 | tf_op jit(solution)/shard_map/slice | solution.py:185
  2.0 2.6 %collective-permute-start = (f32[2,32,2048]{2,1,0:T(8,128)S(1)}, f32[2,32,2048]{2,1,0:T(8,128)S(1)}, u32[]{:S(2)}, u32[]{:S(2)}) collective-permute-start(f32[2,32,2048]{2,1,0:T(8,128)S(1)} %get-tuple-element.162), channel_id=1, source_target_pairs={{0,16},{16,0},{32,48},{48,32},{64,80},{80,64},{96,112},{112,96},{1... | collective-permute-start | bytes 1572872 | tf_op jit(solution)/shard_map/ppermute | solution.py:187
  6.7 29.2 %conditional.1 = (f32[64,128]{1,0:T(8,128)S(1)}, f32[64,128]{1,0:T(8,128)S(1)}, f32[64,128]{1,0:T(8,128)S(1)}, f32[2,112,128]{2,1,0:T(8,128)S(1)}, f32[2,8,2048]...) conditional(s32[]{:T(128)} %convert_element_type.71, ...), branch_computations={%region_2.3_spmd, %region_3.4_spmd} | conditional | flops 559650 | bytes 12644571 | solution.py:209
  7.5 1.0 copy.12
  8.5 10.8 %all-to-all-start = ((f32[16,64,128]{2,1,0:T(8,128)}), f32[16,64,128]{2,1,0:T(8,128)S(1)}, u32[]{:S(2)}, u32[]{:S(2)}) async-start(f32[16,64,128]{2,1,0:T(8,128)} %copy.12), calls=%async_computation | async-start | bytes 1048576 | tf_op jit(solution)/shard_map/cond/branch_0_fun/all_to_all | solution.py:199
  26.5 0.7 fusion.12
  27.2 0.9 fusion.3
  28.2 7.4 %all-to-all-done = f32[16,64,128]{2,1,0:T(8,128)S(1)} async-done(((f32[16,64,128]{2,1,0:T(8,128)}), f32[16,64,128]{2,1,0:T(8,128)S(1)}, u32[]{:S(2)}, u32[]{:S(2)}) %all-to-all-start) | async-done | bytes 524320 | tf_op jit(solution)/shard_map/cond/branch_0_fun/all_to_all | solution.py:199
  36.3 7.0 %collective-permute-start.1 = (f32[36,128]{1,0:T(8,128)S(1)}, f32[36,128]{1,0:T(8,128)S(1)}, u32[]{:S(2)}, u32[]{:S(2)}) collective-permute-start(f32[36,128]{1,0:T(8,128)S(1)} %broadcast_select_fusion.3), channel_id=1, source_target_pairs={{1,16},{2,17},{3,18},{4,19},{5,20},{6,21},{7,22},{8,23},{9,24},{10... | collective-permute-start | bytes 55304 | tf_op jit(solution)/shard_map/ppermute | solution.py:228
  43.4 1.7 %collective-permute-done.1 = f32[36,128]{1,0:T(8,128)S(1)} collective-permute-done((f32[36,128]{1,0:T(8,128)S(1)}, f32[36,128]{1,0:T(8,128)S(1)}, u32[]{:S(2)}, u32[]{:S(2)}) %collective-permute-start.1) | collective-permute-done | bytes 18464 | tf_op jit(solution)/shard_map/ppermute | solution.py:228
  45.0 0.9 broadcast_in_dim.52
  45.9 4.0 %all-to-all-start.2 = ((f32[8,160,128]{2,1,0:T(8,128)}), f32[8,160,128]{2,1,0:T(8,128)S(1)}, u32[]{:S(2)}, u32[]{:S(2)}) async-start(f32[8,160,128]{2,1,0:T(8,128)} %broadcast_in_dim.52), calls=%async_computation.2 | async-start | bytes 1310720 | tf_op jit(solution)/shard_map/all_to_all | solution.py:241
  50.0 20.7 %all-to-all-done.2.refs_3_.refs_2_ = f32[8,160,128]{2,1,0:T(8,128)S(1)} async-done(((f32[8,160,128]{2,1,0:T(8,128)}), f32[8,160,128]{2,1,0:T(8,128)S(1)}, u32[]{:S(2)}, u32[]{:S(2)}) %all-to-all-start.2) | async-done | bytes 655392 | tf_op jit(solution)/shard_map/all_to_all | solution.py:241
  70.8 2.2 %collective-permute-start.2 = (f32[8,160,128]{2,1,0:T(8,128)S(1)}, f32[8,160,128]{2,1,0:T(8,128)S(1)}, u32[]{:S(2)}, u32[]{:S(2)}) collective-permute-start(f32[8,160,128]{2,1,0:T(8,128)S(1)} %all-to-all-done.2.refs_3_.refs_2_), channel_id=1, source_target_pairs={{0,32},{16,48},{32,0},{48,16},{64,96},{80,112},{96,64},{112,80},{1... | collective-permute-start | bytes 1966088 | tf_op jit(solution)/shard_map/ppermute | solution.py:248
  73.1 14.4 %all_to_all.18.refs_2_ = f32[8,72,128]{2,1,0:T(8,128)S(1)} all-to-all(f32[8,72,128]{2,1,0:T(8,128)S(1)} %broadcast_in_dim.53), channel_id=1, replica_groups={{0,64,128,192,256,320,384,448},{16,80,144,208,272,336,400,464},{32,96,1..., dimensions={0} | all-to-all | bytes 589824 | tf_op jit(solution)/shard_map/all_to_all | solution.py:241
  87.5 1.0 collective-permute-done.2.refs_4_.refs_3_
  88.5 1.2 %pad_maximum_fusion.2 = f32[2,8,160,128]{3,2,1,0:T(8,128)} fusion(f32[1,8,160,128]{3,2,1,0:T(8,128)S(1)} %bitcast.95, f32[1,8,160,128]{3,2,1,0:T(8,128)S(1)} %bitcast.94), kind=kLoop, calls=%fused_computation.80 | loop fusion | flops 327680 | bytes 2621440 | tf_op jit(solution)/shard_map/stack | solution.py:244
  89.7 3.2 %collective-permute-start.4 = (f32[2,8,160,128]{3,2,1,0:T(8,128)}, f32[2,8,160,128]{3,2,1,0:T(8,128)S(1)}, u32[]{:S(2)}, u32[]{:S(2)}) collective-permute-start(f32[2,8,160,128]{3,2,1,0:T(8,128)} %pad_maximum_fusion.2), channel_id=1, source_target_pairs={{0,16},{16,0},{32,48},{48,32},{64,80},{80,64},{96,112},{112,96},{1... | collective-permute-start | bytes 3932168 | tf_op jit(solution)/shard_map/ppermute | solution.py:244
  92.9 2.3 %collective-permute-start.3 = (f32[8,72,128]{2,1,0:T(8,128)S(1)}, f32[8,72,128]{2,1,0:T(8,128)S(1)}, u32[]{:S(2)}, u32[]{:S(2)}) collective-permute-start(f32[8,72,128]{2,1,0:T(8,128)S(1)} %all_to_all.18.refs_2_), channel_id=1, source_target_pairs={{0,32},{16,48},{32,0},{48,16},{64,96},{80,112},{96,64},{112,80},{1... | collective-permute-start | bytes 884744 | tf_op jit(solution)/shard_map/ppermute | solution.py:251
  95.7 4.4 %shard_map.50.refs_1_ = f32[2,112,2048]{2,1,0:T(8,128)S(1)} custom-call(s32[4]{0:T(128)S(1)} %pad_add_fusion.refs_0_, f32[2,112,128]{2,1,0:T(8,128)S(1)} %get-tuple-element.104.refs_1_, f32[2,8,2048]{2,1,0:T(8,128)S(1)} %get-tuple-element.105.refs_2_, f32[8,160,128]{2,1,0:T(8,128)S(1)} %all-to-all-done.2.refs_3_.refs_2_, ...), custom_call_target="tpu_custom_call" | custom-call | flops 20000000 | bytes 6000000 | tf_op jit(solution)/shard_map/pallas_call | solution.py:262
  100.1 4.0 %shard_map.51.refs_1_ = f32[2,112,2048]{2,1,0:T(8,128)S(1)} custom-call(s32[4]{0:T(128)S(1)} %pad_add_fusion.refs_0_, f32[2,112,2048]{2,1,0:T(8,128)S(1)} %shard_map.50.refs_1_, f32[8,160,128]{2,1,0:T(8,128)S(1)} %all-to-all-done.2.refs_3_.refs_2_, f32[8,160,128]{2,1,0:T(8,128)S(1)} %collective-permute-done.2.refs_4_.refs_3_, ...), custom_call_target="tpu_custom_call" | custom-call | flops 20000000 | bytes 6000000 | tf_op jit(solution)/shard_map/pallas_call | solution.py:262
  104.1 2.3 %collective-permute-start.5 = (f32[2,8,72,128]{3,2,1,0:T(8,128)S(1)}, f32[2,8,72,128]{3,2,1,0:T(8,128)S(1)}, u32[]{:S(2)}, u32[]{:S(2)}) collective-permute-start(f32[2,8,72,128]{3,2,1,0:T(8,128)S(1)} %pad_maximum_fusion.3), channel_id=1, source_target_pairs={{0,16},{16,0},{32,48},{48,32},{64,80},{80,64},{96,112},{112,96},{1... | collective-permute-start | bytes 1769480 | tf_op jit(solution)/shard_map/ppermute | solution.py:244
  106.4 1.6 %collective-permute-done.5.refs_4_ = f32[2,8,72,128]{3,2,1,0:T(8,128)S(1)} collective-permute-done((f32[2,8,72,128]{3,2,1,0:T(8,128)S(1)}, f32[2,8,72,128]{3,2,1,0:T(8,128)S(1)}, u32[]{:S(2)}, u32[]{:S(2)}) %collective-permute-start.5) | collective-permute-done | bytes 589856 | tf_op jit(solution)/shard_map/ppermute | solution.py:244
  108.0 4.6 %shard_map.52 = (f32[1,64,2048]{2,1,0:T(8,128)}, f32[1,64,2048]{2,1,0:T(8,128)}) custom-call(s32[4]{0:T(128)S(1)} %pad_add_fusion.refs_0_, f32[2,112,2048]{2,1,0:T(8,128)S(1)} %shard_map.51.refs_1_, f32[8,72,128]{2,1,0:T(8,128)S(1)} %all_to_all.18.refs_2_, f32[8,72,128]{2,1,0:T(8,128)S(1)} %collective-permute-done.3.refs_3_, ...), custom_call_target="tpu_custom_call" | custom-call | flops 20000000 | bytes 6000000 | tf_op jit(solution)/shard_map/pallas_call | solution.py:262
  (37 shorter events, 4.3 us)
Async XLA Ops:
  0.6 4.0 %copy-start = (s32[3]{0:T(128)S(1)}, s32[3]{0:T(128)}, u32[]{:S(2)}) copy-start(s32[3]{0:T(128)} %param.6) | copy-start | bytes 40
  0.7 6.0 %copy-start.1 = (s32[1,2]{1,0:T(1,128)S(1)}, s32[1,2]{1,0:T(1,128)}, u32[]{:S(2)}) copy-start(s32[1,2]{1,0:T(1,128)} %param.7) | copy-start | bytes 28
  2.0 4.6 %collective-permute-start = (f32[2,32,2048]{2,1,0:T(8,128)S(1)}, f32[2,32,2048]{2,1,0:T(8,128)S(1)}, u32[]{:S(2)}, u32[]{:S(2)}) collective-permute-start(f32[2,32,2048]{2,1,0:T(8,128)S(1)} %get-tuple-element.162), channel_id=1, source_target_pairs={{0,16},{16,0},{32,48},{48,32},{64,80},{80,64},{96,112},{112,96},{1... | collective-permute-start | bytes 1572872 | tf_op jit(solution)/shard_map/ppermute | solution.py:187
  8.5 27.1 %all-to-all-start = ((f32[16,64,128]{2,1,0:T(8,128)}), f32[16,64,128]{2,1,0:T(8,128)S(1)}, u32[]{:S(2)}, u32[]{:S(2)}) async-start(f32[16,64,128]{2,1,0:T(8,128)} %copy.12), calls=%async_computation | async-start | bytes 1048576 | tf_op jit(solution)/shard_map/cond/branch_0_fun/all_to_all | solution.py:199
  36.3 8.7 %collective-permute-start.1 = (f32[36,128]{1,0:T(8,128)S(1)}, f32[36,128]{1,0:T(8,128)S(1)}, u32[]{:S(2)}, u32[]{:S(2)}) collective-permute-start(f32[36,128]{1,0:T(8,128)S(1)} %broadcast_select_fusion.3), channel_id=1, source_target_pairs={{1,16},{2,17},{3,18},{4,19},{5,20},{6,21},{7,22},{8,23},{9,24},{10... | collective-permute-start | bytes 55304 | tf_op jit(solution)/shard_map/ppermute | solution.py:228
  45.9 24.8 %all-to-all-start.2 = ((f32[8,160,128]{2,1,0:T(8,128)}), f32[8,160,128]{2,1,0:T(8,128)S(1)}, u32[]{:S(2)}, u32[]{:S(2)}) async-start(f32[8,160,128]{2,1,0:T(8,128)} %broadcast_in_dim.52), calls=%async_computation.2 | async-start | bytes 1310720 | tf_op jit(solution)/shard_map/all_to_all | solution.py:241
  70.8 17.8 %collective-permute-start.2 = (f32[8,160,128]{2,1,0:T(8,128)S(1)}, f32[8,160,128]{2,1,0:T(8,128)S(1)}, u32[]{:S(2)}, u32[]{:S(2)}) collective-permute-start(f32[8,160,128]{2,1,0:T(8,128)S(1)} %all-to-all-done.2.refs_3_.refs_2_), channel_id=1, source_target_pairs={{0,32},{16,48},{32,0},{48,16},{64,96},{80,112},{96,64},{112,80},{1... | collective-permute-start | bytes 1966088 | tf_op jit(solution)/shard_map/ppermute | solution.py:248
  89.7 6.0 %collective-permute-start.4 = (f32[2,8,160,128]{3,2,1,0:T(8,128)}, f32[2,8,160,128]{3,2,1,0:T(8,128)S(1)}, u32[]{:S(2)}, u32[]{:S(2)}) collective-permute-start(f32[2,8,160,128]{3,2,1,0:T(8,128)} %pad_maximum_fusion.2), channel_id=1, source_target_pairs={{0,16},{16,0},{32,48},{48,32},{64,80},{80,64},{96,112},{112,96},{1... | collective-permute-start | bytes 3932168 | tf_op jit(solution)/shard_map/ppermute | solution.py:244
  92.9 11.2 %collective-permute-start.3 = (f32[8,72,128]{2,1,0:T(8,128)S(1)}, f32[8,72,128]{2,1,0:T(8,128)S(1)}, u32[]{:S(2)}, u32[]{:S(2)}) collective-permute-start(f32[8,72,128]{2,1,0:T(8,128)S(1)} %all_to_all.18.refs_2_), channel_id=1, source_target_pairs={{0,32},{16,48},{32,0},{48,16},{64,96},{80,112},{96,64},{112,80},{1... | collective-permute-start | bytes 884744 | tf_op jit(solution)/shard_map/ppermute | solution.py:251
  104.1 3.9 %collective-permute-start.5 = (f32[2,8,72,128]{3,2,1,0:T(8,128)S(1)}, f32[2,8,72,128]{3,2,1,0:T(8,128)S(1)}, u32[]{:S(2)}, u32[]{:S(2)}) collective-permute-start(f32[2,8,72,128]{3,2,1,0:T(8,128)S(1)} %pad_maximum_fusion.3), channel_id=1, source_target_pairs={{0,16},{16,0},{32,48},{48,32},{64,80},{80,64},{96,112},{112,96},{1... | collective-permute-start | bytes 1769480 | tf_op jit(solution)/shard_map/ppermute | solution.py:244

commit v5 on v4

--- a/solution.py
+++ b/solution.py
@@ -85,7 +85,7 @@
             ref[TOP + 64 : ROWS, :] = jnp.zeros((ROWS - TOP - 64, ref.shape[1]), jnp.float32)
 
 
-def advance(place, s, plane_ref, field, trial, after, cols):
+def advance(place, s, plane_ref, field, trial, after, cols, done=None):
     row = lax.broadcasted_iota(jnp.int32, (8, LANES), 0)
     lane = lax.broadcasted_iota(jnp.int32, (8, LANES), 1)
 
@@ -116,6 +116,8 @@
             span = slice(c * LANES, (c + 1) * LANES)
             old = field[0, at, span] + re[c]
             after[0][0][to, span] = 0.5 * old - (0.5 * diffraction) * b[c]
+        if done is not None:
+            done(i - after[1])
         return carry
 
     lax.fori_loop(*TRIAL[s], first, 0, unroll=True)
@@ -143,6 +145,7 @@
     waves = [refs.pop(0) for _ in range(2)] if first else []
     before = None if first else refs.pop(0)
     mine, other, theirs = refs[:3]
+    sent, exits = (refs.pop(), refs.pop()) if last else (None, None)
     planes, trial, field = refs[-3:]
     assemble(place, (mine, other), (theirs.at[0], theirs.at[1]), planes, slab, place_in, cols)
     if first:
@@ -152,7 +155,22 @@
     advance(place, 2 * slab, planes.at[0], before, trial, (middle, 0), cols)
     clear_outside(place, middle)
     if last:
-        advance(place, 2 * slab + 1, planes.at[1], field, trial, ((refs[3].at[0], refs[4].at[0]), TOP // 8), cols)
+
+        def copies(i):
+            at = pl.ds(pl.multiple_of(i * 8, 8), 8)
+            return [
+                pltpu.make_async_copy(exits.at[part, at, :], refs[3 + part].at[0, at, :], sent.at[part, i])
+                for part in range(2)
+            ]
+
+        def done(i):
+            for copy in copies(i):
+                copy.start()
+
+        advance(place, 2 * slab + 1, planes.at[1], field, trial, ((exits.at[0], exits.at[1]), TOP // 8), cols, done)
+        for i in range(8):
+            for copy in copies(i):
+                copy.wait()
     else:
         after = refs[3].at[0], refs[3].at[1]
         advance(place, 2 * slab + 1, planes.at[1], field, trial, (after, 0), cols)
@@ -270,12 +288,13 @@
             ),
             out_shape=(out, out) if end else state,
             in_specs=[pl.BlockSpec(memory_space=pltpu.SMEM)] + [in_vmem] * (len(before) + len(pieces)),
-            out_specs=(in_vmem, in_vmem) if end else in_vmem,
+            out_specs=(pl.BlockSpec(memory_space=pl.ANY),) * 2 if end else in_vmem,
             scratch_shapes=[
                 pltpu.VMEM((depth, ROWS, cols), jnp.float32),
                 pltpu.VMEM(state.shape, jnp.float32),
                 pltpu.VMEM(state.shape, jnp.float32),
-            ],
+            ]
+            + ([pltpu.VMEM((2, rows, cols), jnp.float32), pltpu.SemaphoreType.DMA((2, 8))] if end else []),
             compiler_params=pltpu.CompilerParams(vmem_limit_bytes=32 * 1024 * 1024),
             cost_estimate=pl.CostEstimate(flops=20_000_000, bytes_accessed=6_000_000, transcendentals=0),
         )(place, *before, *pieces)

time: 113 us -> 113 us (level)
  no operation moved by 1% of the time
where the time goes in v5:
time: 113 us
  starting transfers between devices  34.3 us (30%)
  waiting for transfers between devices  33 us (29%)
  blocking collectives  14.4 us (13%)
  Pallas kernels  12.8 us (11%)
  loops' own time  6.71 us (6%)
  other arithmetic  5.86 us (5%)
  local copies, waits for them, and re-layouts  3.97 us (4%)
  between operations  1.66 us (1%)
    all_to_all x1, waiting for transfers between devices, along_z(): lax.all_to_all(copies, 'ang', 0, 0, tiled=True, axis_index_groups=columns)  20.7 us
    all_to_all x1, blocking collectives, along_z(): lax.all_to_all(copies, 'ang', 0, 0, tiled=True, axis_index_groups=columns)  14.4 us
    pallas_call x3, Pallas kernels, step(): pl.pallas_call(functools.partial(through, slab=slab, place_in=(rows * cho...  12.8 us
    all_to_all x1, starting transfers between devices, one(): lax.all_to_all(tiles, 'ang', 0, 0, tiled=True, axis_index_groups=by_chip)  10.8 us
    all_to_all x1, waiting for transfers between devices, one(): lax.all_to_all(tiles, 'ang', 0, 0, tiled=True, axis_index_groups=by_chip)  7.41 us
    ppermute x1, starting transfers between devices, per_device(): edge = lax.ppermute(edge, ('ang', 'xy'), up + [(j, i) for i, j in up])  7.04 us
    another operation x1, loops' own time, keep(): return lax.cond(shared, both, one)  6.71 us
    ppermute x2, starting transfers between devices, from_core(): return lax.ppermute(jnp.stack([mine, other]), 'ang', swap_core)  5.43 us
  transfers between devices with their start and end apart: 8, of which 6 were waited for; matrix products, arithmetic and copies ran while one was open for 4% of the time, Pallas kernels for 7%

profile of v5, /device:TPU:29, one launch (start us, length us, event | category | flops | bytes accessed | tf_op | source)
XLA Modules:
  0.0 112.6 jit_solution(625559502261028428)
XLA Ops:
  0.7 1.4 %fusion.33 = (f32[2,32,2048]{2,1,0:T(8,128)S(1)}, f32[2,32,2048]{2,1,0:T(8,128)S(1)}, f32[2,32,2048]{2,1,0:T(8,128)S(1)}) fusion(f32[2,64,2048]{2,1,0:T(8,128)} %bitcast.111, pred[]{:T(512)} %eq.42), kind=kLoop, calls=%fused_computation.99 | loop fusion | flops 131072 | bytes 2621441 | tf_op jit(solution)/shard_map/slice | solution.py:203
  2.0 2.6 %collective-permute-start = (f32[2,32,2048]{2,1,0:T(8,128)S(1)}, f32[2,32,2048]{2,1,0:T(8,128)S(1)}, u32[]{:S(2)}, u32[]{:S(2)}) collective-permute-start(f32[2,32,2048]{2,1,0:T(8,128)S(1)} %get-tuple-element.162), channel_id=1, source_target_pairs={{0,16},{16,0},{32,48},{48,32},{64,80},{80,64},{96,112},{112,96},{1... | collective-permute-start | bytes 1572872 | tf_op jit(solution)/shard_map/ppermute | solution.py:205
  6.7 29.2 %conditional.1 = (f32[64,128]{1,0:T(8,128)S(1)}, f32[64,128]{1,0:T(8,128)S(1)}, f32[64,128]{1,0:T(8,128)S(1)}, f32[2,112,128]{2,1,0:T(8,128)S(1)}, f32[2,8,2048]...) conditional(s32[]{:T(128)} %convert_element_type.71, ...), branch_computations={%region_2.3_spmd, %region_3.4_spmd} | conditional | flops 559650 | bytes 12644571 | solution.py:227
  7.5 1.0 copy.12
  8.5 10.8 %all-to-all-start = ((f32[16,64,128]{2,1,0:T(8,128)}), f32[16,64,128]{2,1,0:T(8,128)S(1)}, u32[]{:S(2)}, u32[]{:S(2)}) async-start(f32[16,64,128]{2,1,0:T(8,128)} %copy.12), calls=%async_computation | async-start | bytes 1048576 | tf_op jit(solution)/shard_map/cond/branch_0_fun/all_to_all | solution.py:217
  26.5 0.7 fusion.12
  27.2 0.9 fusion.3
  28.2 7.4 %all-to-all-done = f32[16,64,128]{2,1,0:T(8,128)S(1)} async-done(((f32[16,64,128]{2,1,0:T(8,128)}), f32[16,64,128]{2,1,0:T(8,128)S(1)}, u32[]{:S(2)}, u32[]{:S(2)}) %all-to-all-start) | async-done | bytes 524320 | tf_op jit(solution)/shard_map/cond/branch_0_fun/all_to_all | solution.py:217
  36.3 7.0 %collective-permute-start.1 = (f32[36,128]{1,0:T(8,128)S(1)}, f32[36,128]{1,0:T(8,128)S(1)}, u32[]{:S(2)}, u32[]{:S(2)}) collective-permute-start(f32[36,128]{1,0:T(8,128)S(1)} %broadcast_select_fusion.3), channel_id=1, source_target_pairs={{1,16},{2,17},{3,18},{4,19},{5,20},{6,21},{7,22},{8,23},{9,24},{10... | collective-permute-start | bytes 55304 | tf_op jit(solution)/shard_map/ppermute | solution.py:246
  43.4 1.7 %collective-permute-done.1 = f32[36,128]{1,0:T(8,128)S(1)} collective-permute-done((f32[36,128]{1,0:T(8,128)S(1)}, f32[36,128]{1,0:T(8,128)S(1)}, u32[]{:S(2)}, u32[]{:S(2)}) %collective-permute-start.1) | collective-permute-done | bytes 18464 | tf_op jit(solution)/shard_map/ppermute | solution.py:246
  45.0 0.9 broadcast_in_dim.52
  45.9 4.0 %all-to-all-start.2 = ((f32[8,160,128]{2,1,0:T(8,128)}), f32[8,160,128]{2,1,0:T(8,128)S(1)}, u32[]{:S(2)}, u32[]{:S(2)}) async-start(f32[8,160,128]{2,1,0:T(8,128)} %broadcast_in_dim.52), calls=%async_computation.2 | async-start | bytes 1310720 | tf_op jit(solution)/shard_map/all_to_all | solution.py:259
  50.0 20.7 %all-to-all-done.2.refs_3_.refs_2_ = f32[8,160,128]{2,1,0:T(8,128)S(1)} async-done(((f32[8,160,128]{2,1,0:T(8,128)}), f32[8,160,128]{2,1,0:T(8,128)S(1)}, u32[]{:S(2)}, u32[]{:S(2)}) %all-to-all-start.2) | async-done | bytes 655392 | tf_op jit(solution)/shard_map/all_to_all | solution.py:259
  70.8 2.2 %collective-permute-start.2 = (f32[8,160,128]{2,1,0:T(8,128)S(1)}, f32[8,160,128]{2,1,0:T(8,128)S(1)}, u32[]{:S(2)}, u32[]{:S(2)}) collective-permute-start(f32[8,160,128]{2,1,0:T(8,128)S(1)} %all-to-all-done.2.refs_3_.refs_2_), channel_id=1, source_target_pairs={{0,32},{16,48},{32,0},{48,16},{64,96},{80,112},{96,64},{112,80},{1... | collective-permute-start | bytes 1966088 | tf_op jit(solution)/shard_map/ppermute | solution.py:266
  73.1 14.4 %all_to_all.18.refs_2_ = f32[8,72,128]{2,1,0:T(8,128)S(1)} all-to-all(f32[8,72,128]{2,1,0:T(8,128)S(1)} %broadcast_in_dim.53), channel_id=1, replica_groups={{0,64,128,192,256,320,384,448},{16,80,144,208,272,336,400,464},{32,96,1..., dimensions={0} | all-to-all | bytes 589824 | tf_op jit(solution)/shard_map/all_to_all | solution.py:259
  87.5 1.0 collective-permute-done.2.refs_4_.refs_3_
  88.5 1.2 %pad_maximum_fusion.2 = f32[2,8,160,128]{3,2,1,0:T(8,128)} fusion(f32[1,8,160,128]{3,2,1,0:T(8,128)S(1)} %bitcast.95, f32[1,8,160,128]{3,2,1,0:T(8,128)S(1)} %bitcast.94), kind=kLoop, calls=%fused_computation.80 | loop fusion | flops 327680 | bytes 2621440 | tf_op jit(solution)/shard_map/stack | solution.py:262
  89.7 3.2 %collective-permute-start.4 = (f32[2,8,160,128]{3,2,1,0:T(8,128)}, f32[2,8,160,128]{3,2,1,0:T(8,128)S(1)}, u32[]{:S(2)}, u32[]{:S(2)}) collective-permute-start(f32[2,8,160,128]{3,2,1,0:T(8,128)} %pad_maximum_fusion.2), channel_id=1, source_target_pairs={{0,16},{16,0},{32,48},{48,32},{64,80},{80,64},{96,112},{112,96},{1... | collective-permute-start | bytes 3932168 | tf_op jit(solution)/shard_map/ppermute | solution.py:262
  92.9 2.3 %collective-permute-start.3 = (f32[8,72,128]{2,1,0:T(8,128)S(1)}, f32[8,72,128]{2,1,0:T(8,128)S(1)}, u32[]{:S(2)}, u32[]{:S(2)}) collective-permute-start(f32[8,72,128]{2,1,0:T(8,128)S(1)} %all_to_all.18.refs_2_), channel_id=1, source_target_pairs={{0,32},{16,48},{32,0},{48,16},{64,96},{80,112},{96,64},{112,80},{1... | collective-permute-start | bytes 884744 | tf_op jit(solution)/shard_map/ppermute | solution.py:269
  95.7 4.4 %shard_map.50.refs_1_ = f32[2,112,2048]{2,1,0:T(8,128)S(1)} custom-call(s32[4]{0:T(128)S(1)} %pad_add_fusion.refs_0_, f32[2,112,128]{2,1,0:T(8,128)S(1)} %get-tuple-element.104.refs_1_, f32[2,8,2048]{2,1,0:T(8,128)S(1)} %get-tuple-element.105.refs_2_, f32[8,160,128]{2,1,0:T(8,128)S(1)} %all-to-all-done.2.refs_3_.refs_2_, ...), custom_call_target="tpu_custom_call" | custom-call | flops 20000000 | bytes 6000000 | tf_op jit(solution)/shard_map/pallas_call | solution.py:280
  100.1 4.0 %shard_map.51.refs_1_ = f32[2,112,2048]{2,1,0:T(8,128)S(1)} custom-call(s32[4]{0:T(128)S(1)} %pad_add_fusion.refs_0_, f32[2,112,2048]{2,1,0:T(8,128)S(1)} %shard_map.50.refs_1_, f32[8,160,128]{2,1,0:T(8,128)S(1)} %all-to-all-done.2.refs_3_.refs_2_, f32[8,160,128]{2,1,0:T(8,128)S(1)} %collective-permute-done.2.refs_4_.refs_3_, ...), custom_call_target="tpu_custom_call" | custom-call | flops 20000000 | bytes 6000000 | tf_op jit(solution)/shard_map/pallas_call | solution.py:280
  104.1 2.3 %collective-permute-start.5 = (f32[2,8,72,128]{3,2,1,0:T(8,128)S(1)}, f32[2,8,72,128]{3,2,1,0:T(8,128)S(1)}, u32[]{:S(2)}, u32[]{:S(2)}) collective-permute-start(f32[2,8,72,128]{3,2,1,0:T(8,128)S(1)} %pad_maximum_fusion.3), channel_id=1, source_target_pairs={{0,16},{16,0},{32,48},{48,32},{64,80},{80,64},{96,112},{112,96},{1... | collective-permute-start | bytes 1769480 | tf_op jit(solution)/shard_map/ppermute | solution.py:262
  106.4 1.6 %collective-permute-done.5.refs_4_ = f32[2,8,72,128]{3,2,1,0:T(8,128)S(1)} collective-permute-done((f32[2,8,72,128]{3,2,1,0:T(8,128)S(1)}, f32[2,8,72,128]{3,2,1,0:T(8,128)S(1)}, u32[]{:S(2)}, u32[]{:S(2)}) %collective-permute-start.5) | collective-permute-done | bytes 589856 | tf_op jit(solution)/shard_map/ppermute | solution.py:262
  108.0 4.4 %shard_map.52 = (f32[1,64,2048]{2,1,0:T(8,128)}, f32[1,64,2048]{2,1,0:T(8,128)}) custom-call(s32[4]{0:T(128)S(1)} %pad_add_fusion.refs_0_, f32[2,112,2048]{2,1,0:T(8,128)S(1)} %shard_map.51.refs_1_, f32[8,72,128]{2,1,0:T(8,128)S(1)} %all_to_all.18.refs_2_, f32[8,72,128]{2,1,0:T(8,128)S(1)} %collective-permute-done.3.refs_3_, ...), custom_call_target="tpu_custom_call" | custom-call | flops 20000000 | bytes 6000000 | tf_op jit(solution)/shard_map/pallas_call | solution.py:280
  (37 shorter events, 4.3 us)
Async XLA Ops:
  0.6 4.0 %copy-start = (s32[3]{0:T(128)S(1)}, s32[3]{0:T(128)}, u32[]{:S(2)}) copy-start(s32[3]{0:T(128)} %param.6) | copy-start | bytes 40
  0.7 6.0 %copy-start.1 = (s32[1,2]{1,0:T(1,128)S(1)}, s32[1,2]{1,0:T(1,128)}, u32[]{:S(2)}) copy-start(s32[1,2]{1,0:T(1,128)} %param.7) | copy-start | bytes 28
  2.0 4.6 %collective-permute-start = (f32[2,32,2048]{2,1,0:T(8,128)S(1)}, f32[2,32,2048]{2,1,0:T(8,128)S(1)}, u32[]{:S(2)}, u32[]{:S(2)}) collective-permute-start(f32[2,32,2048]{2,1,0:T(8,128)S(1)} %get-tuple-element.162), channel_id=1, source_target_pairs={{0,16},{16,0},{32,48},{48,32},{64,80},{80,64},{96,112},{112,96},{1... | collective-permute-start | bytes 1572872 | tf_op jit(solution)/shard_map/ppermute | solution.py:205
  8.5 27.1 %all-to-all-start = ((f32[16,64,128]{2,1,0:T(8,128)}), f32[16,64,128]{2,1,0:T(8,128)S(1)}, u32[]{:S(2)}, u32[]{:S(2)}) async-start(f32[16,64,128]{2,1,0:T(8,128)} %copy.12), calls=%async_computation | async-start | bytes 1048576 | tf_op jit(solution)/shard_map/cond/branch_0_fun/all_to_all | solution.py:217
  36.3 8.7 %collective-permute-start.1 = (f32[36,128]{1,0:T(8,128)S(1)}, f32[36,128]{1,0:T(8,128)S(1)}, u32[]{:S(2)}, u32[]{:S(2)}) collective-permute-start(f32[36,128]{1,0:T(8,128)S(1)} %broadcast_select_fusion.3), channel_id=1, source_target_pairs={{1,16},{2,17},{3,18},{4,19},{5,20},{6,21},{7,22},{8,23},{9,24},{10... | collective-permute-start | bytes 55304 | tf_op jit(solution)/shard_map/ppermute | solution.py:246
  45.9 24.8 %all-to-all-start.2 = ((f32[8,160,128]{2,1,0:T(8,128)}), f32[8,160,128]{2,1,0:T(8,128)S(1)}, u32[]{:S(2)}, u32[]{:S(2)}) async-start(f32[8,160,128]{2,1,0:T(8,128)} %broadcast_in_dim.52), calls=%async_computation.2 | async-start | bytes 1310720 | tf_op jit(solution)/shard_map/all_to_all | solution.py:259
  70.8 17.8 %collective-permute-start.2 = (f32[8,160,128]{2,1,0:T(8,128)S(1)}, f32[8,160,128]{2,1,0:T(8,128)S(1)}, u32[]{:S(2)}, u32[]{:S(2)}) collective-permute-start(f32[8,160,128]{2,1,0:T(8,128)S(1)} %all-to-all-done.2.refs_3_.refs_2_), channel_id=1, source_target_pairs={{0,32},{16,48},{32,0},{48,16},{64,96},{80,112},{96,64},{112,80},{1... | collective-permute-start | bytes 1966088 | tf_op jit(solution)/shard_map/ppermute | solution.py:266
  89.7 6.0 %collective-permute-start.4 = (f32[2,8,160,128]{3,2,1,0:T(8,128)}, f32[2,8,160,128]{3,2,1,0:T(8,128)S(1)}, u32[]{:S(2)}, u32[]{:S(2)}) collective-permute-start(f32[2,8,160,128]{3,2,1,0:T(8,128)} %pad_maximum_fusion.2), channel_id=1, source_target_pairs={{0,16},{16,0},{32,48},{48,32},{64,80},{80,64},{96,112},{112,96},{1... | collective-permute-start | bytes 3932168 | tf_op jit(solution)/shard_map/ppermute | solution.py:262
  92.9 11.2 %collective-permute-start.3 = (f32[8,72,128]{2,1,0:T(8,128)S(1)}, f32[8,72,128]{2,1,0:T(8,128)S(1)}, u32[]{:S(2)}, u32[]{:S(2)}) collective-permute-start(f32[8,72,128]{2,1,0:T(8,128)S(1)} %all_to_all.18.refs_2_), channel_id=1, source_target_pairs={{0,32},{16,48},{32,0},{48,16},{64,96},{80,112},{96,64},{112,80},{1... | collective-permute-start | bytes 884744 | tf_op jit(solution)/shard_map/ppermute | solution.py:269
  104.1 3.9 %collective-permute-start.5 = (f32[2,8,72,128]{3,2,1,0:T(8,128)S(1)}, f32[2,8,72,128]{3,2,1,0:T(8,128)S(1)}, u32[]{:S(2)}, u32[]{:S(2)}) collective-permute-start(f32[2,8,72,128]{3,2,1,0:T(8,128)S(1)} %pad_maximum_fusion.3), channel_id=1, source_target_pairs={{0,16},{16,0},{32,48},{48,32},{64,80},{80,64},{96,112},{112,96},{1... | collective-permute-start | bytes 1769480 | tf_op jit(solution)/shard_map/ppermute | solution.py:262
